TPU v7x, 128 devices: a whole 4x4x4 slice. The times are simulated.
128 devices in a mesh: slab: 8 (over y, z_lo), plane: 16 (over x, z_hi, core).
Axes of the slice: x: 4, y: 4, z: 4 (z_hi: 2, z_lo: 2; z = z_hi * 2 + z_lo), core: 2. Of those that a mesh axis runs over, the one named last changes fastest.
Arguments:
- right_sides: float32 [8, 256, 32768], P('slab', 'plane'), may hold values from -6 to 6
- diag_tiles: bfloat16 [8, 2, 32768, 2048], P('slab', None, 'plane'), may hold values from -0.09375 to 0.09375
- left_factors: bfloat16 [8, 2, 96, 32768], P('slab', None, None, 'plane'), may hold values from -0.4375 to 0.4375
- source_factors: bfloat16 [8, 2, 96, 32768], P('slab', None, None, 'plane'), may hold values from -0.0234375 to 0.0234375
- trace_factors: bfloat16 [8, 2, 96, 32768], P('slab', None, None, 'plane'), may hold values from -0.01953125 to 0.01953125
Outputs:
- solved: float32 [8, 256, 32768], P('slab', 'plane')
All inputs are finite; a program needn't handle non-finite values.
Results may differ from a plain program's by a relative error of at most 0.0029.
Values may be sent and summed in bfloat16 or wider, within the bound.
A program may use at most 128 MiB of HBM per device.

v0:
```python
import jax
import jax.numpy as jnp
from jax import lax
from jax.sharding import PartitionSpec as P


def from_behind(block, axis, distance):
    devices = range(lax.axis_size(axis))
    route = [(i - distance, i) for i in devices if i - distance in devices]
    return lax.ppermute(block, axis, route)


def combine_parts(real_part, imag_part):
    half_count = real_part.shape[0] // 2
    upper_rows = real_part[:half_count] - imag_part[half_count:]
    lower_rows = real_part[half_count:] + imag_part[:half_count]
    return jnp.concatenate([upper_rows, lower_rows], axis=0)


def complex_apply(vectors, mat_real, mat_imag, contract_axis, precision):
    contract = (((1,), (contract_axis,)), ((), ()))
    real_part = lax.dot_general(
        vectors, mat_real, contract, precision=precision, preferred_element_type=jnp.float32
    )
    imag_part = lax.dot_general(
        vectors, mat_imag, contract, precision=precision, preferred_element_type=jnp.float32
    )
    return combine_parts(real_part, imag_part)


def body(right_sides, diag_tiles, left_factors, source_factors, trace_factors):
    precise = lax.Precision.HIGHEST
    half_sides = right_sides.astype(jnp.bfloat16)
    regrouped = lax.all_to_all(half_sides, "plane", split_axis=2, concat_axis=1, tiled=True)[0]
    local_part = complex_apply(regrouped, diag_tiles[0, 0], diag_tiles[0, 1], 1, None)
    source_term = complex_apply(regrouped, source_factors[0, 0], source_factors[0, 1], 1, None)
    trace_real = trace_factors[0, 0].astype(jnp.float32)
    trace_imag = trace_factors[0, 1].astype(jnp.float32)
    left_real = left_factors[0, 0].astype(jnp.float32)
    left_imag = left_factors[0, 1].astype(jnp.float32)
    incoming = jnp.zeros_like(local_part)
    solved = local_part
    for step_index in range(lax.axis_size("slab")):
        if step_index > 0:
            incoming = from_behind(solved, "slab", 1)
        partial_value = source_term + complex_apply(incoming, trace_real, trace_imag, 1, precise)
        mixing = lax.psum(partial_value, "plane")
        solved = local_part + complex_apply(mixing, left_real, left_imag, 0, precise)
    return lax.all_to_all(solved[None], "plane", split_axis=1, concat_axis=2, tiled=True)


def solution(mesh):
    placed = (
        P("slab", "plane", None),
        P("slab", None, "plane", None),
        P("slab", None, None, "plane"),
        P("slab", None, None, "plane"),
        P("slab", None, None, "plane"),
    )
    return jax.shard_map(
        body, mesh=mesh, in_specs=placed, out_specs=P("slab", "plane", None), check_vma=False
    )
```

profile of v0, /device:TPU:25, one launch (start us, length us, event | category | flops | bytes accessed | tf_op | source)
XLA Modules:
  0.0 1779.5 jit_solution(11900252239563247781)
XLA Ops:
  6.5 1.7 convert_element_type.2
  8.2 25.0 %copy.10 = bf16[1,16,32768]{1,0,2:T(2,128)(2,1)} copy(bf16[1,16,32768]{2,1,0:T(8,128)(2,1)S(1)} %convert_element_type.2) | data formatting | bytes 2097152 | tf_op jit(solution)/shard_map/convert_element_type | solution.py:33
  33.7 179.2 %reduce = bf16[32768,16]{1,0:T(8,128)(2,1)} reduce(bf16[32768,1,16]{2,1,0:T(2,128)(2,1)} %bitcast.124, bf16[]{:T(256)} %broadcast), dimensions={1}, to_apply=%bitcast.85.reduce_sub_computation | reduce | bytes 2097154
  212.9 11.3 reshape.56
  224.3 8.3 all-to-all-start
  233.7 16.1 all-to-all-done
  249.8 14.1 reshape.57
  263.9 29.6 %copy.11 = bf16[1,16,32768]{2,1,0:T(8,128)(2,1)S(1)} copy(bf16[1,16,32768]{1,0,2:T(2,128)(2,1)} %bitcast.125) | data formatting | bytes 2097152 | tf_op jit(solution)/shard_map/all_to_all | solution.py:34
  296.2 7.1 fusion
  303.3 7.1 fusion.2
  311.1 2.6 slice_subtract_fusion.8
  313.7 125.6 %all-reduce.9.cloned.1.call-done = f32[256,96]{0,1:T(8,128)} async-done(((f32[256,96]{0,1:T(8,128)}), f32[256,96]{0,1:T(8,128)}) %all-reduce.9.cloned.1.call-update) | async-done | bytes 98320 | tf_op jit(solution)/shard_map/psum | solution.py:47
  439.3 2.0 fusion.26
  441.3 1.0 fusion.42
  442.8 2.5 collective-permute-start
  445.4 45.4 %collective-permute-done = f32[256,2048]{1,0:T(8,128)S(1)} collective-permute-done((f32[256,2048]{1,0:T(8,128)S(1)}, f32[256,2048]{1,0:T(8,128)S(1)}, u32[]{:S(2)}, u32[]{:S(2)}) %collective-permute-start) | collective-permute-done | bytes 2097184 | tf_op jit(solution)/shard_map/ppermute | solution.py:10
  490.8 1.2 fusion.56
  492.0 1.2 fusion.63
  494.0 129.7 %all-reduce.11.cloned.1.call-done = f32[256,96]{0,1:T(8,128)} async-done(((f32[256,96]{0,1:T(8,128)}), f32[256,96]{0,1:T(8,128)}) %all-reduce.11.cloned.1.call-update) | async-done | bytes 98320 | tf_op jit(solution)/shard_map/psum | solution.py:47
  623.7 2.0 fusion.24
  627.3 2.3 collective-permute-start.1
  629.6 45.6 %collective-permute-done.1 = f32[256,2048]{1,0:T(8,128)S(1)} collective-permute-done((f32[256,2048]{1,0:T(8,128)S(1)}, f32[256,2048]{1,0:T(8,128)S(1)}, u32[]{:S(2)}, u32[]{:S(2)}) %collective-permute-start.1) | collective-permute-done | bytes 2097184 | tf_op jit(solution)/shard_map/ppermute | solution.py:10
  675.2 1.2 fusion.55
  676.5 1.2 fusion.62
  678.5 129.7 %all-reduce.13.cloned.1.call-done = f32[256,96]{0,1:T(8,128)} async-done(((f32[256,96]{0,1:T(8,128)}), f32[256,96]{0,1:T(8,128)}) %all-reduce.13.cloned.1.call-update) | async-done | bytes 98320 | tf_op jit(solution)/shard_map/psum | solution.py:47
  808.2 2.0 fusion.22
  810.2 1.0 fusion.38
  811.8 2.3 collective-permute-start.2
  814.0 45.6 %collective-permute-done.2 = f32[256,2048]{1,0:T(8,128)S(1)} collective-permute-done((f32[256,2048]{1,0:T(8,128)S(1)}, f32[256,2048]{1,0:T(8,128)S(1)}, u32[]{:S(2)}, u32[]{:S(2)}) %collective-permute-start.2) | collective-permute-done | bytes 2097184 | tf_op jit(solution)/shard_map/ppermute | solution.py:10
  859.7 1.2 fusion.54
  860.9 1.2 fusion.61
  863.4 129.3 %all-reduce.15.cloned.1.call-done = f32[256,96]{0,1:T(8,128)} async-done(((f32[256,96]{0,1:T(8,128)}), f32[256,96]{0,1:T(8,128)}) %all-reduce.15.cloned.1.call-update) | async-done | bytes 98320 | tf_op jit(solution)/shard_map/psum | solution.py:47
  992.6 2.0 fusion.20
  994.6 1.0 fusion.36
  996.2 2.3 collective-permute-start.3
  998.5 45.6 %collective-permute-done.3 = f32[256,2048]{1,0:T(8,128)S(1)} collective-permute-done((f32[256,2048]{1,0:T(8,128)S(1)}, f32[256,2048]{1,0:T(8,128)S(1)}, u32[]{:S(2)}, u32[]{:S(2)}) %collective-permute-start.3) | collective-permute-done | bytes 2097184 | tf_op jit(solution)/shard_map/ppermute | solution.py:10
  1044.1 1.2 fusion.53
  1045.4 1.2 fusion.60
  1047.4 129.7 %all-reduce.17.cloned.1.call-done = f32[256,96]{0,1:T(8,128)} async-done(((f32[256,96]{0,1:T(8,128)}), f32[256,96]{0,1:T(8,128)}) %all-reduce.17.cloned.1.call-update) | async-done | bytes 98320 | tf_op jit(solution)/shard_map/psum | solution.py:47
  1177.1 2.0 fusion.18
  1180.7 2.3 collective-permute-start.4
  1183.0 45.6 %collective-permute-done.4 = f32[256,2048]{1,0:T(8,128)S(1)} collective-permute-done((f32[256,2048]{1,0:T(8,128)S(1)}, f32[256,2048]{1,0:T(8,128)S(1)}, u32[]{:S(2)}, u32[]{:S(2)}) %collective-permute-start.4) | collective-permute-done | bytes 2097184 | tf_op jit(solution)/shard_map/ppermute | solution.py:10
  1228.6 1.2 fusion.52
  1229.8 1.2 fusion.59
  1231.8 129.7 %all-reduce.19.cloned.1.call-done = f32[256,96]{0,1:T(8,128)} async-done(((f32[256,96]{0,1:T(8,128)}), f32[256,96]{0,1:T(8,128)}) %all-reduce.19.cloned.1.call-update) | async-done | bytes 98320 | tf_op jit(solution)/shard_map/psum | solution.py:47
  1361.5 2.0 fusion.16
  1363.5 1.0 fusion.32
  1365.1 2.5 collective-permute-start.5
  1367.6 45.5 %collective-permute-done.5 = f32[256,2048]{1,0:T(8,128)S(1)} collective-permute-done((f32[256,2048]{1,0:T(8,128)S(1)}, f32[256,2048]{1,0:T(8,128)S(1)}, u32[]{:S(2)}, u32[]{:S(2)}) %collective-permute-start.5) | collective-permute-done | bytes 2097184 | tf_op jit(solution)/shard_map/ppermute | solution.py:10
  1413.1 1.2 fusion.51
  1414.3 1.2 fusion.58
  1416.3 129.7 %all-reduce.21.cloned.1.call-done = f32[256,96]{0,1:T(8,128)} async-done(((f32[256,96]{0,1:T(8,128)}), f32[256,96]{0,1:T(8,128)}) %all-reduce.21.cloned.1.call-update) | async-done | bytes 98320 | tf_op jit(solution)/shard_map/psum | solution.py:47
  1546.0 2.0 fusion.14
  1548.0 1.0 fusion.30
  1549.6 2.3 collective-permute-start.6
  1551.9 45.6 %collective-permute-done.6 = f32[256,2048]{1,0:T(8,128)S(1)} collective-permute-done((f32[256,2048]{1,0:T(8,128)S(1)}, f32[256,2048]{1,0:T(8,128)S(1)}, u32[]{:S(2)}, u32[]{:S(2)}) %collective-permute-start.6) | collective-permute-done | bytes 2097184 | tf_op jit(solution)/shard_map/ppermute | solution.py:10
  1597.5 1.2 fusion.50
  1598.7 1.2 fusion.57
  1600.7 129.8 %all-reduce.23.cloned.1.call-done = f32[256,96]{0,1:T(8,128)} async-done(((f32[256,96]{0,1:T(8,128)}), f32[256,96]{0,1:T(8,128)}) %all-reduce.23.cloned.1.call-update) | async-done | bytes 98320 | tf_op jit(solution)/shard_map/psum | solution.py:47
  1730.5 2.0 fusion.12
  1734.0 2.2 copy.13
  1736.2 33.5 %all_to_all.33 = f32[1,256,2048]{2,0,1:T(1,128)S(1)} all-to-all(f32[1,256,2048]{2,0,1:T(1,128)S(1)} %copy.13), channel_id=1, replica_groups=mesh['slab'=8,'plane'=16] {'plane'}, dimensions={1} | all-to-all | bytes 4194304 | tf_op jit(solution)/shard_map/all_to_all | solution.py:49
  1769.7 1.2 copy.14
  1770.9 1.5 all_to_all.30
  (95 shorter events, 17.7 us)
Async XLA Ops:
  212.9 19.8 %copy-start.1 = (bf16[1,2,96,2048]{3,2,1,0:T(8,128)(2,1)S(1)}, bf16[1,2,96,2048]{3,2,1,0:T(8,128)(2,1)}, u32[]{:S(2)}) copy-start(bf16[1,2,96,2048]{3,2,1,0:T(8,128)(2,1)} %param.9) | copy-start | bytes 2359300
  224.3 25.5 %all-to-all-start = ((bf16[16,2,16384]{2,1,0:T(2,128)(2,1)}), bf16[16,2,16384]{2,1,0:T(2,128)(2,1)S(1)}, u32[]{:S(2)}, u32[]{:S(2)}) async-start(bf16[16,2,16384]{2,1,0:T(2,128)(2,1)} %reshape.56), calls=%async_computation | async-start | bytes 2097152 | tf_op jit(solution)/shard_map/all_to_all | solution.py:34
  232.6 206.7 %all-reduce.9.cloned.1.call-start = ((), (), s32[]{:S(2)}) async-start(), calls=%async_computation.2 | async-start | bytes 196608 | tf_op jit(solution)/shard_map/psum | solution.py:47
  294.1 1.1 copy-start.9
  311.0 128.2 %copy-start = (bf16[1,2,96,2048]{3,2,1,0:T(8,128)(2,1)S(1)}, bf16[1,2,96,2048]{3,2,1,0:T(8,128)(2,1)}, u32[]{:S(2)}) copy-start(bf16[1,2,96,2048]{3,2,1,0:T(8,128)(2,1)} %param.7) | copy-start | bytes 2359300
  311.1 312.7 %all-reduce.11.cloned.1.call-start = ((), (), s32[]{:S(2)}) async-start(), calls=%async_computation.3 | async-start | bytes 196608 | tf_op jit(solution)/shard_map/psum | solution.py:47
  439.3 2.0 copy-start.10
  442.6 48.2 %copy-start.2 = (bf16[1,2,96,2048]{3,2,1,0:T(8,128)(2,1)S(1)}, bf16[1,2,96,2048]{3,2,1,0:T(8,128)(2,1)}, u32[]{:S(2)}) copy-start(bf16[1,2,96,2048]{3,2,1,0:T(8,128)(2,1)} %param.9) | copy-start | bytes 2359300
  442.8 47.9 %collective-permute-start = (f32[256,2048]{1,0:T(8,128)S(1)}, f32[256,2048]{1,0:T(8,128)S(1)}, u32[]{:S(2)}, u32[]{:S(2)}) collective-permute-start(f32[256,2048]{1,0:T(8,128)S(1)} %maximum_add_fusion.1), channel_id=1, source_target_pairs={{0,16},{16,32},{32,48},{48,64},{64,80},{80,96},{96,112},{1,17},{17... | collective-permute-start | bytes 6291464 | tf_op jit(solution)/shard_map/ppermute | solution.py:10
  493.9 314.2 %all-reduce.13.cloned.1.call-start = ((), (), s32[]{:S(2)}) async-start(), calls=%async_computation.4 | async-start | bytes 196608 | tf_op jit(solution)/shard_map/psum | solution.py:47
  623.7 2.0 copy-start.11
  627.0 48.2 %copy-start.3 = (bf16[1,2,96,2048]{3,2,1,0:T(8,128)(2,1)S(1)}, bf16[1,2,96,2048]{3,2,1,0:T(8,128)(2,1)}, u32[]{:S(2)}) copy-start(bf16[1,2,96,2048]{3,2,1,0:T(8,128)(2,1)} %param.9) | copy-start | bytes 2359300
  627.3 47.9 %collective-permute-start.1 = (f32[256,2048]{1,0:T(8,128)S(1)}, f32[256,2048]{1,0:T(8,128)S(1)}, u32[]{:S(2)}, u32[]{:S(2)}) collective-permute-start(f32[256,2048]{1,0:T(8,128)S(1)} %maximum_add_fusion.2), channel_id=1, source_target_pairs={{0,16},{16,32},{32,48},{48,64},{64,80},{80,96},{96,112},{1,17},{17... | collective-permute-start | bytes 6291464 | tf_op jit(solution)/shard_map/ppermute | solution.py:10
  678.4 314.2 %all-reduce.15.cloned.1.call-start = ((), (), s32[]{:S(2)}) async-start(), calls=%async_computation.5 | async-start | bytes 196608 | tf_op jit(solution)/shard_map/psum | solution.py:47
  808.2 2.0 copy-start.12
  811.5 48.2 %copy-start.4 = (bf16[1,2,96,2048]{3,2,1,0:T(8,128)(2,1)S(1)}, bf16[1,2,96,2048]{3,2,1,0:T(8,128)(2,1)}, u32[]{:S(2)}) copy-start(bf16[1,2,96,2048]{3,2,1,0:T(8,128)(2,1)} %param.9) | copy-start | bytes 2359300
  811.8 47.9 %collective-permute-start.2 = (f32[256,2048]{1,0:T(8,128)S(1)}, f32[256,2048]{1,0:T(8,128)S(1)}, u32[]{:S(2)}, u32[]{:S(2)}) collective-permute-start(f32[256,2048]{1,0:T(8,128)S(1)} %maximum_add_fusion.3), channel_id=1, source_target_pairs={{0,16},{16,32},{32,48},{48,64},{64,80},{80,96},{96,112},{1,17},{17... | collective-permute-start | bytes 6291464 | tf_op jit(solution)/shard_map/ppermute | solution.py:10
  862.9 314.2 %all-reduce.17.cloned.1.call-start = ((), (), s32[]{:S(2)}) async-start(), calls=%async_computation.6 | async-start | bytes 196608 | tf_op jit(solution)/shard_map/psum | solution.py:47
  992.6 2.0 copy-start.13
  995.9 48.2 %copy-start.5 = (bf16[1,2,96,2048]{3,2,1,0:T(8,128)(2,1)S(1)}, bf16[1,2,96,2048]{3,2,1,0:T(8,128)(2,1)}, u32[]{:S(2)}) copy-start(bf16[1,2,96,2048]{3,2,1,0:T(8,128)(2,1)} %param.9) | copy-start | bytes 2359300
  996.2 47.9 %collective-permute-start.3 = (f32[256,2048]{1,0:T(8,128)S(1)}, f32[256,2048]{1,0:T(8,128)S(1)}, u32[]{:S(2)}, u32[]{:S(2)}) collective-permute-start(f32[256,2048]{1,0:T(8,128)S(1)} %maximum_add_fusion.4), channel_id=1, source_target_pairs={{0,16},{16,32},{32,48},{48,64},{64,80},{80,96},{96,112},{1,17},{17... | collective-permute-start | bytes 6291464 | tf_op jit(solution)/shard_map/ppermute | solution.py:10
  1047.3 314.2 %all-reduce.19.cloned.1.call-start = ((), (), s32[]{:S(2)}) async-start(), calls=%async_computation.7 | async-start | bytes 196608 | tf_op jit(solution)/shard_map/psum | solution.py:47
  1177.1 2.0 copy-start.14
  1180.4 48.2 %copy-start.6 = (bf16[1,2,96,2048]{3,2,1,0:T(8,128)(2,1)S(1)}, bf16[1,2,96,2048]{3,2,1,0:T(8,128)(2,1)}, u32[]{:S(2)}) copy-start(bf16[1,2,96,2048]{3,2,1,0:T(8,128)(2,1)} %param.9) | copy-start | bytes 2359300
  1180.7 47.9 %collective-permute-start.4 = (f32[256,2048]{1,0:T(8,128)S(1)}, f32[256,2048]{1,0:T(8,128)S(1)}, u32[]{:S(2)}, u32[]{:S(2)}) collective-permute-start(f32[256,2048]{1,0:T(8,128)S(1)} %maximum_add_fusion.5), channel_id=1, source_target_pairs={{0,16},{16,32},{32,48},{48,64},{64,80},{80,96},{96,112},{1,17},{17... | collective-permute-start | bytes 6291464 | tf_op jit(solution)/shard_map/ppermute | solution.py:10
  1231.8 314.2 %all-reduce.21.cloned.1.call-start = ((), (), s32[]{:S(2)}) async-start(), calls=%async_computation.8 | async-start | bytes 196608 | tf_op jit(solution)/shard_map/psum | solution.py:47
  1361.5 2.0 copy-start.15
  1364.9 48.2 %copy-start.7 = (bf16[1,2,96,2048]{3,2,1,0:T(8,128)(2,1)S(1)}, bf16[1,2,96,2048]{3,2,1,0:T(8,128)(2,1)}, u32[]{:S(2)}) copy-start(bf16[1,2,96,2048]{3,2,1,0:T(8,128)(2,1)} %param.9) | copy-start | bytes 2359300
  1365.1 47.9 %collective-permute-start.5 = (f32[256,2048]{1,0:T(8,128)S(1)}, f32[256,2048]{1,0:T(8,128)S(1)}, u32[]{:S(2)}, u32[]{:S(2)}) collective-permute-start(f32[256,2048]{1,0:T(8,128)S(1)} %maximum_add_fusion.6), channel_id=1, source_target_pairs={{0,16},{16,32},{32,48},{48,64},{64,80},{80,96},{96,112},{1,17},{17... | collective-permute-start | bytes 6291464 | tf_op jit(solution)/shard_map/ppermute | solution.py:10
  1416.2 314.2 %all-reduce.23.cloned.1.call-start = ((), (), s32[]{:S(2)}) async-start(), calls=%async_computation.9 | async-start | bytes 196608 | tf_op jit(solution)/shard_map/psum | solution.py:47
  1546.0 2.0 copy-start.16
  1549.3 48.2 %copy-start.8 = (bf16[1,2,96,2048]{3,2,1,0:T(8,128)(2,1)S(1)}, bf16[1,2,96,2048]{3,2,1,0:T(8,128)(2,1)}, u32[]{:S(2)}) copy-start(bf16[1,2,96,2048]{3,2,1,0:T(8,128)(2,1)} %param.9) | copy-start | bytes 2359300
  1549.6 47.9 %collective-permute-start.6 = (f32[256,2048]{1,0:T(8,128)S(1)}, f32[256,2048]{1,0:T(8,128)S(1)}, u32[]{:S(2)}, u32[]{:S(2)}) collective-permute-start(f32[256,2048]{1,0:T(8,128)S(1)} %maximum_add_fusion.7), channel_id=1, source_target_pairs={{0,16},{16,32},{32,48},{48,64},{64,80},{80,96},{96,112},{1,17},{17... | collective-permute-start | bytes 6291464 | tf_op jit(solution)/shard_map/ppermute | solution.py:10
  1730.4 2.0 copy-start.17
Sparse Core Ops, SparseCore 0:
  311.2 128.0 all-reduce.8
  494.1 129.6 all-reduce.10
  678.5 129.6 all-reduce.12
  863.0 129.6 all-reduce.14
  1047.4 129.6 all-reduce.16
  1231.9 129.6 all-reduce.18
  1416.3 129.6 all-reduce.20
  1600.8 129.6 all-reduce.22
where the time goes:
time: 1790 us; the launch traced here: 1780 us
  waiting for transfers between devices  1370 us (77%)
  other arithmetic  193 us (11%)
  local copies, waits for them, and re-layouts  87.3 us (5%)
  matrix products  57.2 us (3%)
  blocking collectives  33.5 us (2%)
  starting transfers between devices  25.6 us (1%)
    psum x8, waiting for transfers between devices, body(): mixing = lax.psum(partial_value, 'plane')  1030 us
    ppermute x7, waiting for transfers between devices, from_behind(): return lax.ppermute(block, axis, route)  319 us
    unnamed x1, other arithmetic  179 us
  transfers between devices with their start and end apart: 16, of which 16 were waited for; matrix products, arithmetic and copies ran while one was open for 0% of the time, Pallas kernels for 0%

commit v1 on v0

v1 whole, which is shorter than its diff:
```python
import functools

import jax
import jax.numpy as jnp
from jax import lax
from jax.experimental import pallas as pl
from jax.experimental.pallas import tpu as pltpu
from jax.sharding import PartitionSpec as P

MESH = pl.DeviceIdType.MESH
F32 = jnp.float32
BF16 = jnp.bfloat16
PAD = 128
CHUNKS = 8
X, T, RM, AM, A1, A2, RS, RP, V1, V2, V4, AV, E = range(13)
N_GROUPS = 13


def split(value):
    high = value.astype(BF16)
    low = (value - high.astype(F32)).astype(BF16)
    return high, low


def nt_dot(rows, mat):
    return lax.dot_general(rows, mat, (((1,), (1,)), ((), ())), preferred_element_type=F32)


def nn_dot(rows, mat):
    return lax.dot_general(rows, mat, (((1,), (0,)), ((), ())), preferred_element_type=F32)


def from_products(both, half):
    real = both[:half, :PAD] - both[half:, PAD:]
    imag = both[half:, :PAD] + both[:half, PAD:]
    return jnp.concatenate([real, imag], axis=1)


def expanded(top):
    real, imag = top[:, :PAD], top[:, PAD:]
    return jnp.concatenate([top, jnp.concatenate([-imag, real], axis=1)], axis=0)


def split_dot(rows, high, low):
    count = rows.shape[0]
    rows_high = rows.astype(BF16).astype(F32)
    stacked = jnp.concatenate([rows_high, rows - rows_high], axis=0).astype(BF16)
    first = nn_dot(stacked, high)
    second = nn_dot(stacked, low)
    return first[:count] + first[count:] + second[:count] + second[count:]


def kernel(
    n_slab, n_plane, rank,
    rs_ref, d_ref, l_ref, sf_ref, t_ref, o_ref,
    d_vm, rs_vm, x_send, x_recv, t_vm, l_vm, s_vm, local, e_send,
    m_part, m_recv, a1, a1_prev, a2, a2_prev, a_high, a_low,
    s_part, s_recv, p_part, p_recv, v_send, v_recv, mix,
    d_sem, rs_sem, in_sem, own_sem, send_sem, recv_sem,
):
    s = lax.axis_index("slab")
    p = lax.axis_index("plane")
    tile = d_ref.shape[2]
    step = tile // CHUNKS
    half = 8 * n_plane

    def remote(src, dst, group, device):
        return pltpu.make_async_remote_copy(
            src_ref=src, dst_ref=dst, send_sem=send_sem.at[group], recv_sem=recv_sem.at[group],
            device_id=device, device_id_type=MESH,
        )

    def await_recv(ref, group):
        remote(ref, ref, group, (s, lax.rem(p + 1, n_plane))).wait_recv()

    def await_send(ref, group):
        remote(ref, ref, group, (s, lax.rem(p + 1, n_plane))).wait_send()

    def to_plane(src_of, dst, group):
        def one(i, carry):
            q = lax.rem(p + i, n_plane)
            remote(src_of(q), dst, group, (s, q)).start()
            return carry
        lax.fori_loop(1, n_plane, one, 0)

    def to_next_slab(src, dst, group):
        def one(i, carry):
            q = lax.rem(p + i, n_plane)
            remote(src.at[q], dst, group, (s + 1, q)).start()
            return carry
        lax.fori_loop(0, n_plane, one, 0)

    def rs_copy(q):
        return pltpu.make_async_copy(
            rs_ref.at[0, :, pl.ds(pl.multiple_of(q * tile, tile), tile)], rs_vm.at[q], rs_sem.at[q]
        )

    def start_rs(i, carry):
        rs_copy(lax.rem(p + i, n_plane)).start()
        return carry
    lax.fori_loop(1, n_plane + 1, start_rs, 0)
    l_copy = pltpu.make_async_copy(l_ref.at[0], l_vm.at[:, pl.ds(0, rank), :], in_sem.at[0])
    s_copy = pltpu.make_async_copy(sf_ref.at[0], s_vm.at[:, pl.ds(0, rank), :], in_sem.at[1])
    l_copy.start()
    s_copy.start()

    def d_copy(j):
        rows = pl.ds(pl.multiple_of(j * step, step), step)
        return pltpu.make_async_copy(d_ref.at[0, :, rows, :], d_vm.at[:, rows, :], d_sem.at[j])

    def start_d(j, carry):
        d_copy(j).start()
        return carry
    lax.fori_loop(0, CHUNKS, start_d, 0)
    for padded in (t_vm, l_vm, s_vm):
        padded[:, rank:, :] = jnp.zeros((2, PAD - rank, tile), BF16)

    barrier = pltpu.get_barrier_semaphore()

    def greet(device):
        pl.semaphore_signal(barrier, inc=1, device_id=device, device_id_type=MESH)

    def greet_plane(i, carry):
        greet((s, lax.rem(p + i, n_plane)))
        return carry
    lax.fori_loop(1, n_plane, greet_plane, 0)
    pl.when(s < n_slab - 1)(lambda: greet((s + 1, p)))
    for distance in (1, 2, 4):
        pl.when(s >= distance)(functools.partial(lambda d: greet((s - d, p)), distance))
    expected = n_plane - 1 + (s >= 1).astype(jnp.int32)
    for distance in (1, 2, 4):
        expected = expected + (s + distance < n_slab).astype(jnp.int32)
    pl.semaphore_wait(barrier, expected)

    t_copy = remote(t_ref.at[0], t_vm.at[:, pl.ds(0, rank), :], T, (s - 1, p))
    pl.when(s >= 1)(t_copy.start)

    def cast_block(q):
        rs_copy(q).wait()
        return rs_vm[q].astype(BF16)

    zbit = lax.rem(p // 2, 2)

    def send_same(i, carry):
        q = lax.rem(p + i, n_plane)
        x_send[q] = cast_block(q)

        @pl.when(lax.rem(q // 2, 2) == zbit)
        def _():
            remote(x_send.at[q], x_recv.at[p], X, (s, q)).start()
        return carry
    lax.fori_loop(1, n_plane, send_same, 0)
    x_recv[p] = cast_block(p)
    pl.when(s >= 1)(t_copy.wait_send)

    def send_other(i, carry):
        q = lax.rem(p + i, n_plane)

        @pl.when(lax.rem(q // 2, 2) != zbit)
        def _():
            remote(x_send.at[q], x_recv.at[p], X, (s, q)).start()
        return carry
    lax.fori_loop(1, n_plane, send_other, 0)

    l_copy.wait()

    @pl.when(s < n_slab - 1)
    def _():
        t_copy.wait_recv()
        products = nt_dot(l_vm[...].reshape(2 * PAD, tile), t_vm[...].reshape(2 * PAD, tile))
        m_part[...] = from_products(products, PAD).reshape(m_part.shape)
        to_next_slab(m_part, m_recv.at[p], RM)

    def keep(index, top):
        square = expanded(top)
        high, low = split(square)
        a_high[index] = high
        a_low[index] = low

    others = pl.ds(0, n_plane - 1)

    @pl.when(s >= 1)
    def _():
        await_recv(m_recv, RM)
        a1[p] = jnp.sum(m_recv[...], axis=0)
        to_plane(lambda q: a1.at[p], a1.at[p], AM)
        await_recv(a1.at[others], AM)
        keep(0, a1[...].reshape(PAD, 2 * PAD))

    a1_copy = remote(a1, a1_prev, A1, (s + 1, p))
    pl.when((s >= 1) & (s < n_slab - 1))(a1_copy.start)

    await_recv(x_recv.at[others], X)
    x = x_recv[...].reshape(2 * half, tile)
    s_copy.wait()
    s_part[...] = from_products(nt_dot(x, s_vm[...].reshape(2 * PAD, tile)), half).reshape(s_part.shape)
    s_recv[p] = s_part[p]
    to_plane(lambda q: s_part.at[q], s_recv.at[p], RS)

    def local_chunk(j, carry):
        d_copy(j).wait()
        rows = pl.ds(pl.multiple_of(j * step, step), step)
        real = nt_dot(x_recv[...].reshape(2 * half, tile), d_vm[0, rows, :])
        imag = nt_dot(x_recv[...].reshape(2 * half, tile), d_vm[1, rows, :])
        local[:half, rows] = real[:half] - imag[half:]
        local[half:, rows] = real[half:] + imag[:half]
        return carry
    lax.fori_loop(0, CHUNKS, local_chunk, 0)

    @pl.when(s < n_slab - 1)
    def _():
        high, low = split(local[...])
        t_rows = t_vm[...].reshape(2 * PAD, tile)
        p_part[...] = from_products(nt_dot(high, t_rows) + nt_dot(low, t_rows), half).reshape(p_part.shape)
        to_next_slab(p_part, p_recv.at[p], RP)

    a2_copy = remote(a2, a2_prev, A2, (s + 2, p))

    @pl.when(s >= 2)
    def _():
        await_recv(a1_prev, A1)
        a2[...] = split_dot(a1_prev[...].reshape(PAD, 2 * PAD), a_high[0], a_low[0]).reshape(a2.shape)
        pl.when(s < n_slab - 2)(a2_copy.start)
        keep(1, a2[...].reshape(PAD, 2 * PAD))

    await_recv(s_recv.at[others], RS)
    v_send[0] = jnp.sum(s_recv[...], axis=0)

    @pl.when(s >= 1)
    def _():
        await_recv(p_recv, RP)
        v_send[0] = v_send[0] + jnp.sum(p_recv[...], axis=0)

    v_copies = []
    for index, (distance, group) in enumerate(((1, V1), (2, V2), (4, V4))):
        copy = remote(v_send.at[index], v_recv.at[index], group, (s + distance, p))
        v_copies.append(copy)
        pl.when(s + distance < n_slab)(copy.start)
        if distance == 4:
            @pl.when(s >= 4)
            def _():
                await_recv(a2_prev, A2)
                top = split_dot(a2_prev[...].reshape(PAD, 2 * PAD), a_high[1], a_low[1])
                keep(2, top)
        v_send[index + 1] = v_send[index]

        @pl.when(s >= distance)
        def _():
            copy.wait_recv()
            v_send[index + 1] = v_send[index] + split_dot(v_recv[index], a_high[index], a_low[index])

    mix[p] = v_send[3]
    to_plane(lambda q: mix.at[p], mix.at[p], AV)
    await_recv(mix.at[others], AV)
    mixing = mix[...].reshape(half, 2 * PAD)
    real, imag = mixing[:, :PAD], mixing[:, PAD:]
    square = jnp.concatenate(
        [jnp.concatenate([real, -imag], axis=1), jnp.concatenate([imag, real], axis=1)], axis=0
    )
    high, low = split(square)
    l_rows = l_vm[...].reshape(2 * PAD, tile)
    solved = local[...] + nn_dot(high, l_rows) + nn_dot(low, l_rows)
    e_send[...] = solved.astype(BF16).reshape(e_send.shape)

    mine = pl.ds(pl.multiple_of(p * tile, tile), tile)
    own = pltpu.make_async_copy(e_send.at[p], o_ref.at[:, mine], own_sem)
    own.start()
    to_plane(lambda q: e_send.at[q], o_ref.at[:, mine], E)
    own.wait()

    await_send(x_send.at[others], X)
    await_send(s_part.at[others], RS)
    await_send(mix.at[others], AV)

    @pl.when(s < n_slab - 1)
    def _():
        await_send(m_part, RM)
        await_send(p_part, RP)

    @pl.when(s >= 1)
    def _():
        await_send(a1.at[others], AM)
        pl.when(s < n_slab - 1)(a1_copy.wait_send)
    pl.when((s >= 2) & (s < n_slab - 2))(a2_copy.wait_send)
    for distance, copy in zip((1, 2, 4), v_copies):
        pl.when(s + distance < n_slab)(copy.wait_send)
    await_send(e_send.at[others], E)
    await_recv(o_ref.at[:, pl.ds(0, (n_plane - 1) * tile)], E)


def solution(mesh):
    n_slab, n_plane = mesh.shape["slab"], mesh.shape["plane"]

    def body(right_sides, diag_tiles, left_factors, source_factors, trace_factors):
        tile, rank = diag_tiles.shape[2], left_factors.shape[2]
        columns = right_sides.shape[1]
        small = pltpu.VMEM((n_plane, 8, 2 * PAD), F32)
        ranks = pltpu.VMEM((n_plane, PAD // n_plane, 2 * PAD), F32)
        padded = pltpu.VMEM((2, PAD, tile), BF16)
        blocks = pltpu.VMEM((n_plane, columns, tile), BF16)
        squares = pltpu.VMEM((3, 2 * PAD, 2 * PAD), BF16)
        out = pl.pallas_call(
            functools.partial(kernel, n_slab, n_plane, rank),
            out_shape=jax.ShapeDtypeStruct((columns, n_plane * tile), BF16),
            in_specs=[pl.BlockSpec(memory_space=pl.ANY)] * 5,
            out_specs=pl.BlockSpec(memory_space=pl.ANY),
            scratch_shapes=[
                pltpu.VMEM((2, tile, tile), BF16),
                pltpu.VMEM((n_plane, columns, tile), F32),
                blocks, blocks, padded, padded, padded,
                pltpu.VMEM((columns * n_plane, tile), F32),
                blocks,
                ranks, ranks, ranks, ranks, ranks, ranks, squares, squares,
                small, small, small, small,
                pltpu.VMEM((4, 8, 2 * PAD), F32),
                pltpu.VMEM((3, 8, 2 * PAD), F32),
                small,
                pltpu.SemaphoreType.DMA((CHUNKS,)),
                pltpu.SemaphoreType.DMA((n_plane,)),
                pltpu.SemaphoreType.DMA((2,)),
                pltpu.SemaphoreType.DMA,
                pltpu.SemaphoreType.DMA((N_GROUPS,)),
                pltpu.SemaphoreType.DMA((N_GROUPS,)),
            ],
            compiler_params=pltpu.CompilerParams(
                collective_id=0, has_side_effects=True, vmem_limit_bytes=60 * 2**20
            ),
            name="sweep",
        )(right_sides, diag_tiles, left_factors, source_factors, trace_factors)
        return out.astype(F32)[None]

    placed = (
        P("slab", "plane", None),
        P("slab", None, "plane", None),
        P("slab", None, None, "plane"),
        P("slab", None, None, "plane"),
        P("slab", None, None, "plane"),
    )
    return jax.shard_map(
        body, mesh=mesh, in_specs=placed, out_specs=P("slab", "plane", None), check_vma=False
    )
```

time: 1790 us -> 98.3 us (0.05)
  waiting for transfers between devices: 1370 us -> 0 us
  other arithmetic: 193 us -> 2.68 us
  Pallas kernels: 0 us -> 93.8 us
  local copies, waits for them, and re-layouts: 87.3 us -> 0 us
  matrix products: 57.2 us -> 0 us
  blocking collectives: 33.5 us -> 0 us
  starting transfers between devices: 25.6 us -> 0 us
    psum x8 -> x0, waiting for transfers between devices: 1030 us -> none  [body(): mixing = lax.psum(partial_value, 'plane')]
    ppermute x7 -> x0, waiting for transfers between devices: 319 us -> none  [from_behind(): return lax.ppermute(block, axis, route)]
    unnamed x1 -> x0, other arithmetic: 179 us -> none
    pallas_call x0 -> x1, Pallas kernels: none -> 93.8 us  [body(): pl.pallas_call(functools.partial(kernel, n_slab, n_plane, rank), out_shap...]
    dot_general x36 -> x0, matrix products: 57.2 us -> none  [the longest x18 32.4 us: complex_apply(): lax.dot_general(vectors, mat_imag, contract, precision=precision, preferr...]
    all_to_all x1 -> x0, blocking collectives: 33.5 us -> none  [body(): lax.all_to_all(solved[None], 'plane', split_axis=1, concat_axis=2, tiled=...]
    all_to_all x5 -> x0, local copies, waits for them, and re-layouts: 33 us -> none  [the longest x3 30.3 us: body(): lax.all_to_all(half_sides, 'plane', split_axis=2, concat_axis=1, tiled=True)]
    unnamed x40 -> x0, local copies, waits for them, and re-layouts: 27.1 us -> none
  transfers between devices with their start and end apart: 16 -> 0, of which waited for: 16 -> 0; matrix products, arithmetic and copies ran while one was open for 0% -> 0% of each run, Pallas kernels for 0% -> 0%
where the time goes in v1:
time: 98.3 us; the launch traced here: 96.5 us
  Pallas kernels  93.8 us (95%)
  other arithmetic  2.68 us (3%)
    pallas_call x1, Pallas kernels, body(): pl.pallas_call(functools.partial(kernel, n_slab, n_plane, rank), out_shap...  93.8 us
    broadcast_in_dim x1, other arithmetic, body(): return out.astype(F32)[None]  2.68 us

profile of v1, /device:TPU:25, one launch (start us, length us, event | category | flops | bytes accessed | tf_op | source)
XLA Modules:
  0.0 96.5 jit_solution(332643421024211730)
XLA Ops:
  0.0 93.8 %sweep.1 = bf16[16,32768]{1,0:T(8,128)(2,1)} custom-call(f32[1,16,32768]{2,1,0:T(8,128)} %rs_ref.1, bf16[1,2,2048,2048]{3,2,1,0:T(8,128)(2,1)} %d_ref.1, bf16[1,2,96,2048]{3,2,1,0:T(8,128)(2,1)} %l_ref.1, bf16[1,2,96,2048]{3,2,1,0:T(8,128)(2,1)} %sf_ref.1, bf16[1,2,96,2048]{3,2,1,0:T(8,128)(2,1)} %t_ref.1), custom_call_target="tpu_custom_call" | custom-call | tf_op jit(solution)/shard_map/sweep/pallas_call | solution.py:302
  93.8 2.7 %bitcast_convert_fusion = f32[1,16,32768]{2,1,0:T(8,128)} fusion(bf16[16,32768]{1,0:T(8,128)(2,1)} %sweep.1), kind=kLoop, calls=%fused_computation | loop fusion | flops 524288 | bytes 3145728 | tf_op jit(solution)/shard_map/broadcast_in_dim | solution.py:330

commit v2 on v1

v2 whole, which is shorter than its diff:
```python
import functools

import jax
import jax.numpy as jnp
from jax import lax
from jax.experimental import pallas as pl
from jax.experimental.pallas import tpu as pltpu
from jax.sharding import PartitionSpec as P

MESH = pl.DeviceIdType.MESH
F32 = jnp.float32
BF16 = jnp.bfloat16
PAD = 128
CHUNKS = 8
X0, X1, T, RM, AM, B1, B2, C2, G2, G4, RS, RP, V1, V2, V3, V4, AV, E = range(18)
N_GROUPS = 18


def split(value):
    high = value.astype(BF16)
    low = (value - high.astype(F32)).astype(BF16)
    return high, low


def nt_dot(rows, mat):
    return lax.dot_general(rows, mat, (((1,), (1,)), ((), ())), preferred_element_type=F32)


def nn_dot(rows, mat):
    return lax.dot_general(rows, mat, (((1,), (0,)), ((), ())), preferred_element_type=F32)


def from_products(both):
    half = both.shape[0] // 2
    real = both[:half, :PAD] - both[half:, PAD:]
    imag = both[half:, :PAD] + both[:half, PAD:]
    return jnp.concatenate([real, imag], axis=1)


def expanded(top):
    real, imag = top[:, :PAD], top[:, PAD:]
    return jnp.concatenate([top, jnp.concatenate([-imag, real], axis=1)], axis=0)


def stacked_halves(rows):
    rows_high = rows.astype(BF16).astype(F32)
    return jnp.concatenate([rows_high, rows - rows_high], axis=0).astype(BF16)


def split_dot(rows, high, low):
    count = rows.shape[0]
    stacked = stacked_halves(rows)
    total = nn_dot(stacked, high) + nn_dot(stacked, low)
    return total[:count] + total[count:]


def kernel(
    n_slab, n_plane, rank,
    rs_ref, d_ref, l_ref, sf_ref, t_ref, o_ref,
    d_vm, rs_vm, x_send, x_recv, t_vm, l_vm, s_vm, local, e_send,
    m_part, m_recv, a1, a2, a4, b1, b2, c2, a_high, a_low,
    s_part, s_recv, p_part, p_recv, v_send, v_recv, mix,
    d_sem, rs_sem, in_sem, own_sem, send_sem, recv_sem,
):
    s = lax.axis_index("slab")
    p = lax.axis_index("plane")
    tile = d_ref.shape[2]
    step = tile // CHUNKS
    side = n_plane // 2
    run = max(1, n_plane // 8)

    def device_at(k):
        slot = lax.rem(k, side)
        return (slot // run) * 2 * run + (k // side) * run + lax.rem(slot, run)

    my_side = lax.rem(p // run, 2)
    my_slot = (p // (2 * run)) * run + lax.rem(p, run)
    far_side = 1 - my_side
    me = my_side * side + my_slot

    def remote(src, dst, group, device):
        return pltpu.make_async_remote_copy(
            src_ref=src, dst_ref=dst, send_sem=send_sem.at[group], recv_sem=recv_sem.at[group],
            device_id=device, device_id_type=MESH,
        )

    peer = (s, lax.rem(p + 1, n_plane))

    def await_recv(ref, group):
        remote(ref, ref, group, peer).wait_recv()

    def await_send(ref, group):
        remote(ref, ref, group, peer).wait_send()

    others = pl.ds(0, n_plane - 1)
    near_others = pl.ds(0, side - 1)
    all_far = pl.ds(0, side)

    def to_plane(src, dst, group):
        def one(i, carry):
            remote(src, dst, group, (s, device_at(lax.rem(me + i, n_plane)))).start()
            return carry
        lax.fori_loop(1, n_plane, one, 0)

    def place(which, i):
        return which * side + lax.rem(my_slot + i, side)

    def blocks_of(which, first, last, src, dst, group, slab):
        def one(i, carry):
            k = place(which, i)
            remote(src.at[k], dst, group, (slab, device_at(k))).start()
            return carry
        lax.fori_loop(first, last, one, 0)

    def rs_copy(k):
        lanes = pl.ds(pl.multiple_of(device_at(k) * tile, tile), tile)
        return pltpu.make_async_copy(rs_ref.at[0, :, lanes], rs_vm.at[k], rs_sem.at[k])

    def start_rs(which):
        def one(i, carry):
            rs_copy(place(which, i)).start()
            return carry
        lax.fori_loop(0, side, one, 0)

    start_rs(my_side)
    s_copy = pltpu.make_async_copy(sf_ref.at[0], s_vm.at[:, pl.ds(0, rank), :], in_sem.at[1])
    s_copy.start()

    def d_copy(j):
        rows = pl.ds(pl.multiple_of(j * step, step), step)
        return pltpu.make_async_copy(d_ref.at[0, :, rows, :], d_vm.at[:, rows, :], d_sem.at[j])

    def start_d(j, carry):
        d_copy(j).start()
        return carry

    v_recv[...] = jnp.zeros_like(v_recv)
    barrier = pltpu.get_barrier_semaphore()

    def greet(device):
        pl.semaphore_signal(barrier, inc=1, device_id=device, device_id_type=MESH)

    def greet_plane(i, carry):
        greet((s, lax.rem(p + i, n_plane)))
        return carry
    lax.fori_loop(1, n_plane, greet_plane, 0)
    pl.when(s < n_slab - 1)(lambda: greet((s + 1, p)))
    for distance in (1, 2, 3, 4):
        pl.when(s >= distance)(functools.partial(lambda d: greet((s - d, p)), distance))

    start_rs(far_side)
    lax.fori_loop(0, CHUNKS, start_d, 0)
    l_copy = pltpu.make_async_copy(l_ref.at[0], l_vm.at[:, pl.ds(0, rank), :], in_sem.at[0])
    l_copy.start()
    for padded in (t_vm, l_vm, s_vm):
        padded[:, rank:, :] = jnp.zeros((2, PAD - rank, tile), BF16)

    a_high[...] = jnp.zeros_like(a_high)
    a_low[...] = jnp.zeros_like(a_low)

    expected = n_plane - 1 + (s >= 1).astype(jnp.int32)
    for distance in (1, 2, 3, 4):
        expected = expected + (s + distance < n_slab).astype(jnp.int32)
    pl.semaphore_wait(barrier, expected)

    t_copy = remote(t_ref.at[0], t_vm.at[:, pl.ds(0, rank), :], T, (s - 1, p))
    pl.when(s >= 1)(t_copy.start)

    def near_block(i, carry):
        k = place(my_side, i)
        rs_copy(k).wait()
        x_send[k] = rs_vm[k].astype(BF16)
        remote(x_send.at[k], x_recv.at[me], X0, (s, device_at(k))).start()
        return carry
    lax.fori_loop(1, side, near_block, 0)
    rs_copy(me).wait()
    x_recv[me] = rs_vm[me].astype(BF16)

    def far_cast(i, carry):
        k = place(far_side, i)
        rs_copy(k).wait()
        x_send[k] = rs_vm[k].astype(BF16)
        return carry
    lax.fori_loop(0, side, far_cast, 0)

    def far_blocks(first, last):
        blocks_of(far_side, first, last, x_send, x_recv.at[me], X1, s)

    def side_rows(which):
        return pl.ds(which * side, side)

    def source_part(which):
        x = x_recv[side_rows(which)].reshape(side * 16, tile)
        products = from_products(nt_dot(x, s_vm[...].reshape(2 * PAD, tile)))
        s_part[side_rows(which)] = products.reshape(side, 8, 2 * PAD)

    def local_part(which, first):
        def chunk(j, carry):
            if first:
                d_copy(j).wait()
            rows = pl.ds(pl.multiple_of(j * step, step), step)
            x = x_recv[side_rows(which)].reshape(side * 16, tile)
            real = nt_dot(x, d_vm[0, rows, :])
            imag = nt_dot(x, d_vm[1, rows, :])
            local[which, :side * 8, rows] = real[:side * 8] - imag[side * 8:]
            local[which, side * 8:, rows] = real[side * 8:] + imag[:side * 8]
            return carry
        lax.fori_loop(0, CHUNKS, chunk, 0)

    def trace_part(which):
        high, low = split(local[which])
        products = nt_dot(jnp.concatenate([high, low], axis=0), t_vm[...].reshape(2 * PAD, tile))
        both = from_products(products[:side * 16] + products[side * 16:])
        p_part[side_rows(which)] = both.reshape(side, 8, 2 * PAD)
        blocks_of(which, 0, side, p_part, p_recv.at[me], RP, s + 1)

    await_recv(x_recv.at[near_others], X0)
    s_copy.wait()
    source_part(my_side)
    s_recv[me] = s_part[me]
    blocks_of(my_side, 1, side, s_part, s_recv.at[me], RS, s)
    local_part(my_side, True)
    l_copy.wait()

    pl.when(s >= 1)(t_copy.wait_send)

    @pl.when(s < n_slab - 1)
    def _():
        t_copy.wait_recv()
        products = nt_dot(l_vm[...].reshape(2 * PAD, tile), t_vm[...].reshape(2 * PAD, tile))
        m_part[...] = from_products(products).reshape(m_part.shape)

        def one(i, carry):
            k = lax.rem(me + i, n_plane)
            remote(m_part.at[k], m_recv.at[me], RM, (s + 1, device_at(k))).start()
            return carry
        lax.fori_loop(0, n_plane, one, 0)

    far_blocks(0, 3 * side // 8)

    def keep(index, top):
        high, low = split(expanded(top.reshape(PAD, 2 * PAD)))
        a_high[index] = high
        a_low[index] = low

    b1_copy = remote(a1.at[me], b1, B1, (s + 1, p))
    b2_copy = remote(a1.at[me], b2, B2, (s + 2, p))
    c2_copy = remote(a2.at[me], c2, C2, (s + 2, p))
    pl.when(s < n_slab - 1)(lambda: trace_part(my_side))

    @pl.when(s >= 1)
    def _():
        await_recv(m_recv, RM)
        a1[me] = jnp.sum(m_recv[...], axis=0)
        to_plane(a1.at[me], a1.at[me], AM)
        pl.when(s + 1 < n_slab)(b1_copy.start)
        pl.when(s + 2 < n_slab)(b2_copy.start)

    far_blocks(3 * side // 8, 6 * side // 8)

    @pl.when(s >= 1)
    def _():
        await_recv(a1.at[others], AM)
        keep(0, a1[...])

    @pl.when(s >= 2)
    def _():
        await_recv(b1, B1)
        a2[me] = split_dot(b1[...], a_high[0], a_low[0])
        to_plane(a2.at[me], a2.at[me], G2)
        pl.when(s + 2 < n_slab)(c2_copy.start)

    far_blocks(6 * side // 8, side)

    @pl.when(s >= 2)
    def _():
        await_recv(a2.at[others], G2)
        keep(1, a2[...])

    @pl.when(s >= 3)
    def _():
        await_recv(b2, B2)
        a4[me, 0] = split_dot(b2[...], a_high[1], a_low[1])
        a4[me, 1] = jnp.zeros(b2.shape, F32)

        @pl.when(s >= 4)
        def _():
            await_recv(c2, C2)
            a4[me, 1] = split_dot(c2[...], a_high[1], a_low[1])
        to_plane(a4.at[me], a4.at[me], G4)

    await_recv(x_recv.at[all_far], X1)
    local_part(far_side, False)
    pl.when(s < n_slab - 1)(lambda: trace_part(far_side))
    source_part(far_side)
    blocks_of(far_side, 0, side, s_part, s_recv.at[me], RS, s)

    @pl.when(s >= 3)
    def _():
        await_recv(a4.at[others], G4)
        keep(2, a4[:, 0])
        keep(3, a4[:, 1])

    await_recv(s_recv.at[others], RS)
    v_send[0] = jnp.sum(s_recv[...], axis=0)

    @pl.when(s >= 1)
    def _():
        await_recv(p_recv, RP)
        v_send[0] = v_send[0] + jnp.sum(p_recv[...], axis=0)

    v_copies = []
    for index, (distance, group) in enumerate(((1, V1), (2, V2), (3, V3), (4, V4))):
        source = v_send.at[0 if distance < 4 else 1]
        v_copies.append(remote(source, v_recv.at[index], group, (s + distance, p)))
    for distance in (1, 2, 3):
        pl.when(s + distance < n_slab)(v_copies[distance - 1].start)
    for distance in (1, 2, 3):
        pl.when(s >= distance)(v_copies[distance - 1].wait_recv)
    total = v_send[0]
    for index in range(3):
        total = total + split_dot(v_recv[index], a_high[index], a_low[index])
    v_send[1] = total
    mix[me] = total
    pl.when(s + 4 < n_slab)(v_copies[3].start)

    @pl.when(s >= 4)
    def _():
        v_copies[3].wait_recv()
        mix[me] = v_send[1] + split_dot(v_recv[3], a_high[3], a_low[3])

    to_plane(mix.at[me], mix.at[me], AV)
    await_recv(mix.at[others], AV)

    mine = pl.ds(pl.multiple_of(p * tile, tile), tile)

    def solve_side(which):
        mixing = mix[side_rows(which)].reshape(side * 8, 2 * PAD)
        real, imag = mixing[:, :PAD], mixing[:, PAD:]
        square = jnp.concatenate(
            [jnp.concatenate([real, -imag], axis=1), jnp.concatenate([imag, real], axis=1)], axis=0
        )
        both = nn_dot(stacked_halves(square), l_vm[...].reshape(2 * PAD, tile))
        solved = local[which] + both[:side * 16] + both[side * 16:]
        e_send[side_rows(which)] = solved.astype(BF16).reshape(side, 16, tile)

    solve_side(far_side)
    blocks_of(far_side, 0, side, e_send, o_ref.at[:, mine], E, s)
    solve_side(my_side)
    blocks_of(my_side, 1, side, e_send, o_ref.at[:, mine], E, s)
    own = pltpu.make_async_copy(e_send.at[me], o_ref.at[:, mine], own_sem)
    own.start()

    await_send(x_send.at[near_others], X0)
    await_send(x_send.at[all_far], X1)
    await_send(s_part.at[others], RS)
    await_send(mix.at[others], AV)

    @pl.when(s < n_slab - 1)
    def _():
        await_send(m_part, RM)
        await_send(p_part, RP)

    @pl.when(s >= 1)
    def _():
        await_send(a1.at[others], AM)
        pl.when(s + 1 < n_slab)(b1_copy.wait_send)
        pl.when(s + 2 < n_slab)(b2_copy.wait_send)

    @pl.when(s >= 2)
    def _():
        await_send(a2.at[others], G2)
        pl.when(s + 2 < n_slab)(c2_copy.wait_send)
    pl.when(s >= 3)(lambda: await_send(a4.at[others], G4))
    for distance in (1, 2, 3, 4):
        pl.when(s + distance < n_slab)(v_copies[distance - 1].wait_send)
    own.wait()
    await_send(e_send.at[others], E)
    await_recv(o_ref.at[:, pl.ds(0, (n_plane - 1) * tile)], E)


def solution(mesh):
    n_slab, n_plane = mesh.shape["slab"], mesh.shape["plane"]

    def body(right_sides, diag_tiles, left_factors, source_factors, trace_factors):
        tile, rank = diag_tiles.shape[2], left_factors.shape[2]
        columns = right_sides.shape[1]
        part = PAD // n_plane
        small = pltpu.VMEM((n_plane, 8, 2 * PAD), F32)
        ranks = pltpu.VMEM((n_plane, part, 2 * PAD), F32)
        one = pltpu.VMEM((part, 2 * PAD), F32)
        padded = pltpu.VMEM((2, PAD, tile), BF16)
        blocks = pltpu.VMEM((n_plane, columns, tile), BF16)
        squares = pltpu.VMEM((4, 2 * PAD, 2 * PAD), BF16)
        out = pl.pallas_call(
            functools.partial(kernel, n_slab, n_plane, rank),
            out_shape=jax.ShapeDtypeStruct((columns, n_plane * tile), BF16),
            in_specs=[pl.BlockSpec(memory_space=pl.ANY)] * 5,
            out_specs=pl.BlockSpec(memory_space=pl.ANY),
            scratch_shapes=[
                pltpu.VMEM((2, tile, tile), BF16),
                pltpu.VMEM((n_plane, columns, tile), F32),
                blocks, blocks, padded, padded, padded,
                pltpu.VMEM((2, columns * n_plane // 2, tile), F32),
                blocks,
                ranks, ranks, ranks, ranks, pltpu.VMEM((n_plane, 2, part, 2 * PAD), F32),
                one, one, one, squares, squares,
                small, small, small, small,
                pltpu.VMEM((2, 8, 2 * PAD), F32),
                pltpu.VMEM((4, 8, 2 * PAD), F32),
                small,
                pltpu.SemaphoreType.DMA((CHUNKS,)),
                pltpu.SemaphoreType.DMA((n_plane,)),
                pltpu.SemaphoreType.DMA((2,)),
                pltpu.SemaphoreType.DMA,
                pltpu.SemaphoreType.DMA((N_GROUPS,)),
                pltpu.SemaphoreType.DMA((N_GROUPS,)),
            ],
            compiler_params=pltpu.CompilerParams(
                collective_id=0, has_side_effects=True, vmem_limit_bytes=60 * 2**20
            ),
            name="sweep",
        )(right_sides, diag_tiles, left_factors, source_factors, trace_factors)
        return out.astype(F32)[None]

    placed = (
        P("slab", "plane", None),
        P("slab", None, "plane", None),
        P("slab", None, None, "plane"),
        P("slab", None, None, "plane"),
        P("slab", None, None, "plane"),
    )
    return jax.shard_map(
        body, mesh=mesh, in_specs=placed, out_specs=P("slab", "plane", None), check_vma=False
    )
```

time: 98.3 us -> 97.2 us (0.989); the launches traced: 96.5 us -> 97.1 us
  no operation moved by 1% of the time
where the time goes in v2:
time: 97.2 us; the launch traced here: 97.1 us
  Pallas kernels  94.4 us (97%)
  other arithmetic  2.68 us (3%)
    pallas_call x1, Pallas kernels, body(): pl.pallas_call(functools.partial(kernel, n_slab, n_plane, rank), out_shap...  94.4 us
    broadcast_in_dim x1, other arithmetic, body(): return out.astype(F32)[None]  2.68 us

profile of v2, /device:TPU:25, one launch (start us, length us, event | category | flops | bytes accessed | tf_op | source)
XLA Modules:
  0.0 97.1 jit_solution(4416310159486777745)
XLA Ops:
  0.0 94.4 %sweep.1 = bf16[16,32768]{1,0:T(8,128)(2,1)} custom-call(f32[1,16,32768]{2,1,0:T(8,128)} %rs_ref.1, bf16[1,2,2048,2048]{3,2,1,0:T(8,128)(2,1)} %d_ref.1, bf16[1,2,96,2048]{3,2,1,0:T(8,128)(2,1)} %l_ref.1, bf16[1,2,96,2048]{3,2,1,0:T(8,128)(2,1)} %sf_ref.1, bf16[1,2,96,2048]{3,2,1,0:T(8,128)(2,1)} %t_ref.1), custom_call_target="tpu_custom_call" | custom-call | tf_op jit(solution)/shard_map/sweep/pallas_call | solution.py:395
  94.4 2.7 %bitcast_convert_fusion = f32[1,16,32768]{2,1,0:T(8,128)} fusion(bf16[16,32768]{1,0:T(8,128)(2,1)} %sweep.1), kind=kLoop, calls=%fused_computation | loop fusion | flops 524288 | bytes 3145728 | tf_op jit(solution)/shard_map/broadcast_in_dim | solution.py:424

commit v3 on v2

--- a/solution.py
+++ b/solution.py
@@ -12,7 +12,7 @@
 BF16 = jnp.bfloat16
 PAD = 128
 CHUNKS = 8
-X0, X1, T, RM, AM, B1, B2, C2, G2, G4, RS, RP, V1, V2, V3, V4, AV, E = range(18)
+X0, X1, T, RM, AM, B1, B2, C2, G2, G4, RS, V1, V2, V3, V4, VB, AV, E = range(18)
 N_GROUPS = 18
 
 
@@ -57,9 +57,9 @@
 def kernel(
     n_slab, n_plane, rank,
     rs_ref, d_ref, l_ref, sf_ref, t_ref, o_ref,
-    d_vm, rs_vm, x_send, x_recv, t_vm, l_vm, s_vm, local, e_send,
+    d_vm, rs_vm, x_send, x_recv, t_vm, l_vm, sw_vm, local, e_send,
     m_part, m_recv, a1, a2, a4, b1, b2, c2, a_high, a_low,
-    s_part, s_recv, p_part, p_recv, v_send, v_recv, mix,
+    c_part, c_recv, u_send, u_recv, v_send, v_recv, mix,
     d_sem, rs_sem, in_sem, own_sem, send_sem, recv_sem,
 ):
     s = lax.axis_index("slab")
@@ -69,14 +69,21 @@
     side = n_plane // 2
     run = max(1, n_plane // 8)
 
+    my_side = lax.rem(lax.div(p, run), 2)
+    my_slot = lax.div(p, 2 * run) * run + lax.rem(p, run)
+    far_side = 1 - my_side
+    me = my_side * side + my_slot
+
+    def place(which, i):
+        return which * side + lax.rem(my_slot + i, side)
+
     def device_at(k):
         slot = lax.rem(k, side)
-        return (slot // run) * 2 * run + (k // side) * run + lax.rem(slot, run)
-
-    my_side = lax.rem(p // run, 2)
-    my_slot = (p // (2 * run)) * run + lax.rem(p, run)
-    far_side = 1 - my_side
-    me = my_side * side + my_slot
+        return lax.div(slot, run) * 2 * run + lax.div(k, side) * run + lax.rem(slot, run)
+
+    by_distance = sorted(range(side), key=lambda i: -min(i, side - i))
+    far = [(k, device_at(k)) for k in (place(far_side, i) for i in by_distance)]
+    near = [(k, device_at(k)) for k in (place(my_side, i) for i in by_distance if i)]
 
     def remote(src, dst, group, device):
         return pltpu.make_async_remote_copy(
@@ -97,20 +104,12 @@
     all_far = pl.ds(0, side)
 
     def to_plane(src, dst, group):
-        def one(i, carry):
-            remote(src, dst, group, (s, device_at(lax.rem(me + i, n_plane)))).start()
-            return carry
-        lax.fori_loop(1, n_plane, one, 0)
-
-    def place(which, i):
-        return which * side + lax.rem(my_slot + i, side)
-
-    def blocks_of(which, first, last, src, dst, group, slab):
-        def one(i, carry):
-            k = place(which, i)
-            remote(src.at[k], dst, group, (slab, device_at(k))).start()
-            return carry
-        lax.fori_loop(first, last, one, 0)
+        for _, q in far + near:
+            remote(src, dst, group, (s, q)).start()
+
+    def blocks_to(targets, src, dst, group, slab):
+        for k, q in targets:
+            remote(src.at[k], dst, group, (slab, q)).start()
 
     def rs_copy(k):
         lanes = pl.ds(pl.multiple_of(device_at(k) * tile, tile), tile)
@@ -123,7 +122,7 @@
         lax.fori_loop(0, side, one, 0)
 
     start_rs(my_side)
-    s_copy = pltpu.make_async_copy(sf_ref.at[0], s_vm.at[:, pl.ds(0, rank), :], in_sem.at[1])
+    s_copy = pltpu.make_async_copy(sf_ref.at[0], sw_vm.at[pl.ds(0, 2), pl.ds(0, rank), :], in_sem.at[1])
     s_copy.start()
 
     def d_copy(j):
@@ -134,7 +133,7 @@
         d_copy(j).start()
         return carry
 
-    v_recv[...] = jnp.zeros_like(v_recv)
+    u_recv[...] = jnp.zeros_like(u_recv)
     barrier = pltpu.get_barrier_semaphore()
 
     def greet(device):
@@ -152,11 +151,15 @@
     lax.fori_loop(0, CHUNKS, start_d, 0)
     l_copy = pltpu.make_async_copy(l_ref.at[0], l_vm.at[:, pl.ds(0, rank), :], in_sem.at[0])
     l_copy.start()
-    for padded in (t_vm, l_vm, s_vm):
-        padded[:, rank:, :] = jnp.zeros((2, PAD - rank, tile), BF16)
+    for padded in (t_vm, l_vm, sw_vm):
+        padded[pl.ds(0, 2), rank:, :] = jnp.zeros((2, PAD - rank, tile), BF16)
 
     a_high[...] = jnp.zeros_like(a_high)
     a_low[...] = jnp.zeros_like(a_low)
+
+    @pl.when(s == n_slab - 1)
+    def _():
+        sw_vm[pl.ds(2, 4)] = jnp.zeros((4, PAD, tile), BF16)
 
     expected = n_plane - 1 + (s >= 1).astype(jnp.int32)
     for distance in (1, 2, 3, 4):
@@ -166,13 +169,10 @@
     t_copy = remote(t_ref.at[0], t_vm.at[:, pl.ds(0, rank), :], T, (s - 1, p))
     pl.when(s >= 1)(t_copy.start)
 
-    def near_block(i, carry):
-        k = place(my_side, i)
+    for k, q in near:
         rs_copy(k).wait()
         x_send[k] = rs_vm[k].astype(BF16)
-        remote(x_send.at[k], x_recv.at[me], X0, (s, device_at(k))).start()
-        return carry
-    lax.fori_loop(1, side, near_block, 0)
+        remote(x_send.at[k], x_recv.at[me], X0, (s, q)).start()
     rs_copy(me).wait()
     x_recv[me] = rs_vm[me].astype(BF16)
 
@@ -183,18 +183,10 @@
         return carry
     lax.fori_loop(0, side, far_cast, 0)
 
-    def far_blocks(first, last):
-        blocks_of(far_side, first, last, x_send, x_recv.at[me], X1, s)
-
     def side_rows(which):
         return pl.ds(which * side, side)
 
-    def source_part(which):
-        x = x_recv[side_rows(which)].reshape(side * 16, tile)
-        products = from_products(nt_dot(x, s_vm[...].reshape(2 * PAD, tile)))
-        s_part[side_rows(which)] = products.reshape(side, 8, 2 * PAD)
-
-    def local_part(which, first):
+    def local_part(which, begin, end, first):
         def chunk(j, carry):
             if first:
                 d_copy(j).wait()
@@ -205,21 +197,34 @@
             local[which, :side * 8, rows] = real[:side * 8] - imag[side * 8:]
             local[which, side * 8:, rows] = real[side * 8:] + imag[:side * 8]
             return carry
-        lax.fori_loop(0, CHUNKS, chunk, 0)
-
-    def trace_part(which):
-        high, low = split(local[which])
-        products = nt_dot(jnp.concatenate([high, low], axis=0), t_vm[...].reshape(2 * PAD, tile))
-        both = from_products(products[:side * 16] + products[side * 16:])
-        p_part[side_rows(which)] = both.reshape(side, 8, 2 * PAD)
-        blocks_of(which, 0, side, p_part, p_recv.at[me], RP, s + 1)
+        lax.fori_loop(begin, end, chunk, 0)
+
+    def trace_weights(first, last):
+        def chunk(j, carry):
+            rows = pl.ds(pl.multiple_of(j * step, step), step)
+            t_rows = t_vm[...].reshape(2 * PAD, tile)
+            with_real = nn_dot(t_rows, d_vm[0, :, rows])
+            with_imag = nn_dot(t_rows, d_vm[1, :, rows])
+            for part, value in enumerate((
+                with_real[:PAD] - with_imag[PAD:], with_imag[:PAD] + with_real[PAD:]
+            )):
+                high, low = split(value)
+                sw_vm[2 + part, :, rows] = high
+                sw_vm[4 + part, :, rows] = low
+            return carry
+        lax.fori_loop(first, last, chunk, 0)
+
+    def rank_part(which):
+        x = x_recv[side_rows(which)].reshape(side * 16, tile)
+        both = nt_dot(x, sw_vm[...].reshape(6 * PAD, tile))
+        source = from_products(both[:, :2 * PAD])
+        trace = from_products(both[:, 2 * PAD:4 * PAD] + both[:, 4 * PAD:])
+        c_part[side_rows(which), 0] = source.reshape(side, 8, 2 * PAD)
+        c_part[side_rows(which), 1] = trace.reshape(side, 8, 2 * PAD)
 
     await_recv(x_recv.at[near_others], X0)
+    local_part(my_side, 0, CHUNKS, True)
     s_copy.wait()
-    source_part(my_side)
-    s_recv[me] = s_part[me]
-    blocks_of(my_side, 1, side, s_part, s_recv.at[me], RS, s)
-    local_part(my_side, True)
     l_copy.wait()
 
     pl.when(s >= 1)(t_copy.wait_send)
@@ -230,13 +235,12 @@
         products = nt_dot(l_vm[...].reshape(2 * PAD, tile), t_vm[...].reshape(2 * PAD, tile))
         m_part[...] = from_products(products).reshape(m_part.shape)
 
-        def one(i, carry):
-            k = lax.rem(me + i, n_plane)
-            remote(m_part.at[k], m_recv.at[me], RM, (s + 1, device_at(k))).start()
-            return carry
-        lax.fori_loop(0, n_plane, one, 0)
-
-    far_blocks(0, 3 * side // 8)
+        blocks_to(far + near + [(me, p)], m_part, m_recv.at[me], RM, s + 1)
+
+    first_batch = 5 * side // 8
+    blocks_to(far[:first_batch], x_send, x_recv.at[me], X1, s)
+    half_chunks = CHUNKS // 2
+    pl.when(s < n_slab - 1)(lambda: trace_weights(0, half_chunks))
 
     def keep(index, top):
         high, low = split(expanded(top.reshape(PAD, 2 * PAD)))
@@ -246,8 +250,6 @@
     b1_copy = remote(a1.at[me], b1, B1, (s + 1, p))
     b2_copy = remote(a1.at[me], b2, B2, (s + 2, p))
     c2_copy = remote(a2.at[me], c2, C2, (s + 2, p))
-    pl.when(s < n_slab - 1)(lambda: trace_part(my_side))
-
     @pl.when(s >= 1)
     def _():
         await_recv(m_recv, RM)
@@ -256,7 +258,8 @@
         pl.when(s + 1 < n_slab)(b1_copy.start)
         pl.when(s + 2 < n_slab)(b2_copy.start)
 
-    far_blocks(3 * side // 8, 6 * side // 8)
+    blocks_to(far[first_batch:], x_send, x_recv.at[me], X1, s)
+    pl.when(s < n_slab - 1)(lambda: trace_weights(half_chunks, CHUNKS))
 
     @pl.when(s >= 1)
     def _():
@@ -270,7 +273,13 @@
         to_plane(a2.at[me], a2.at[me], G2)
         pl.when(s + 2 < n_slab)(c2_copy.start)
 
-    far_blocks(6 * side // 8, side)
+    rank_part(my_side)
+    c_recv[me] = c_part[me]
+    blocks_to(near, c_part, c_recv.at[me], RS, s)
+
+    await_recv(x_recv.at[all_far], X1)
+    rank_part(far_side)
+    blocks_to(far, c_part, c_recv.at[me], RS, s)
 
     @pl.when(s >= 2)
     def _():
@@ -289,11 +298,15 @@
             a4[me, 1] = split_dot(c2[...], a_high[1], a_low[1])
         to_plane(a4.at[me], a4.at[me], G4)
 
-    await_recv(x_recv.at[all_far], X1)
-    local_part(far_side, False)
-    pl.when(s < n_slab - 1)(lambda: trace_part(far_side))
-    source_part(far_side)
-    blocks_of(far_side, 0, side, s_part, s_recv.at[me], RS, s)
+    local_part(far_side, 0, half_chunks, False)
+    await_recv(c_recv.at[others], RS)
+    u_send[...] = jnp.sum(c_recv[...], axis=0)
+    u_copies = []
+    for index, group in enumerate((V1, V2, V3, V4)):
+        copy = remote(u_send, u_recv.at[index], group, (s + index + 1, p))
+        u_copies.append(copy)
+        pl.when(s + index + 1 < n_slab)(copy.start)
+    local_part(far_side, half_chunks, CHUNKS, False)
 
     @pl.when(s >= 3)
     def _():
@@ -301,33 +314,20 @@
         keep(2, a4[:, 0])
         keep(3, a4[:, 1])
 
-    await_recv(s_recv.at[others], RS)
-    v_send[0] = jnp.sum(s_recv[...], axis=0)
-
-    @pl.when(s >= 1)
-    def _():
-        await_recv(p_recv, RP)
-        v_send[0] = v_send[0] + jnp.sum(p_recv[...], axis=0)
-
-    v_copies = []
-    for index, (distance, group) in enumerate(((1, V1), (2, V2), (3, V3), (4, V4))):
-        source = v_send.at[0 if distance < 4 else 1]
-        v_copies.append(remote(source, v_recv.at[index], group, (s + distance, p)))
-    for distance in (1, 2, 3):
-        pl.when(s + distance < n_slab)(v_copies[distance - 1].start)
-    for distance in (1, 2, 3):
-        pl.when(s >= distance)(v_copies[distance - 1].wait_recv)
-    total = v_send[0]
+    for index in range(4):
+        pl.when(s > index)(u_copies[index].wait_recv)
+    total = u_send[0] + u_recv[0, 1]
     for index in range(3):
-        total = total + split_dot(v_recv[index], a_high[index], a_low[index])
-    v_send[1] = total
+        total = total + split_dot(u_recv[index, 0] + u_recv[index + 1, 1], a_high[index], a_low[index])
+    v_send[...] = total
     mix[me] = total
-    pl.when(s + 4 < n_slab)(v_copies[3].start)
+    v_copy = remote(v_send, v_recv, VB, (s + 4, p))
+    pl.when(s + 4 < n_slab)(v_copy.start)
 
     @pl.when(s >= 4)
     def _():
-        v_copies[3].wait_recv()
-        mix[me] = v_send[1] + split_dot(v_recv[3], a_high[3], a_low[3])
+        v_copy.wait_recv()
+        mix[me] = v_send[...] + split_dot(v_recv[...], a_high[3], a_low[3])
 
     to_plane(mix.at[me], mix.at[me], AV)
     await_recv(mix.at[others], AV)
@@ -345,21 +345,20 @@
         e_send[side_rows(which)] = solved.astype(BF16).reshape(side, 16, tile)
 
     solve_side(far_side)
-    blocks_of(far_side, 0, side, e_send, o_ref.at[:, mine], E, s)
+    blocks_to(far, e_send, o_ref.at[:, mine], E, s)
     solve_side(my_side)
-    blocks_of(my_side, 1, side, e_send, o_ref.at[:, mine], E, s)
+    blocks_to(near, e_send, o_ref.at[:, mine], E, s)
     own = pltpu.make_async_copy(e_send.at[me], o_ref.at[:, mine], own_sem)
     own.start()
 
     await_send(x_send.at[near_others], X0)
     await_send(x_send.at[all_far], X1)
-    await_send(s_part.at[others], RS)
+    await_send(c_part.at[others], RS)
     await_send(mix.at[others], AV)
 
     @pl.when(s < n_slab - 1)
     def _():
         await_send(m_part, RM)
-        await_send(p_part, RP)
 
     @pl.when(s >= 1)
     def _():
@@ -372,8 +371,9 @@
         await_send(a2.at[others], G2)
         pl.when(s + 2 < n_slab)(c2_copy.wait_send)
     pl.when(s >= 3)(lambda: await_send(a4.at[others], G4))
-    for distance in (1, 2, 3, 4):
-        pl.when(s + distance < n_slab)(v_copies[distance - 1].wait_send)
+    for index in range(4):
+        pl.when(s + index + 1 < n_slab)(u_copies[index].wait_send)
+    pl.when(s + 4 < n_slab)(v_copy.wait_send)
     own.wait()
     await_send(e_send.at[others], E)
     await_recv(o_ref.at[:, pl.ds(0, (n_plane - 1) * tile)], E)
@@ -386,7 +386,7 @@
         tile, rank = diag_tiles.shape[2], left_factors.shape[2]
         columns = right_sides.shape[1]
         part = PAD // n_plane
-        small = pltpu.VMEM((n_plane, 8, 2 * PAD), F32)
+        pairs = pltpu.VMEM((n_plane, 2, 8, 2 * PAD), F32)
         ranks = pltpu.VMEM((n_plane, part, 2 * PAD), F32)
         one = pltpu.VMEM((part, 2 * PAD), F32)
         padded = pltpu.VMEM((2, PAD, tile), BF16)
@@ -400,15 +400,17 @@
             scratch_shapes=[
                 pltpu.VMEM((2, tile, tile), BF16),
                 pltpu.VMEM((n_plane, columns, tile), F32),
-                blocks, blocks, padded, padded, padded,
+                blocks, blocks, padded, padded, pltpu.VMEM((6, PAD, tile), BF16),
                 pltpu.VMEM((2, columns * n_plane // 2, tile), F32),
                 blocks,
                 ranks, ranks, ranks, ranks, pltpu.VMEM((n_plane, 2, part, 2 * PAD), F32),
                 one, one, one, squares, squares,
-                small, small, small, small,
+                pairs, pairs,
                 pltpu.VMEM((2, 8, 2 * PAD), F32),
-                pltpu.VMEM((4, 8, 2 * PAD), F32),
-                small,
+                pltpu.VMEM((4, 2, 8, 2 * PAD), F32),
+                pltpu.VMEM((8, 2 * PAD), F32),
+                pltpu.VMEM((8, 2 * PAD), F32),
+                pltpu.VMEM((n_plane, 8, 2 * PAD), F32),
                 pltpu.SemaphoreType.DMA((CHUNKS,)),
                 pltpu.SemaphoreType.DMA((n_plane,)),
                 pltpu.SemaphoreType.DMA((2,)),

time: 97.2 us -> 83.5 us (0.86); the launches traced: 97.1 us -> 82.1 us
  Pallas kernels: 94.4 us -> 79.4 us
    pallas_call x1, Pallas kernels: 94.4 us -> 79.4 us  [body(): pl.pallas_call(functools.partial(kernel, n_slab, n_plane, rank), out_shap...]
where the time goes in v3:
time: 83.5 us; the launch traced here: 82.1 us
  Pallas kernels  79.4 us (95%)
  other arithmetic  2.68 us (3%)
    pallas_call x1, Pallas kernels, body(): pl.pallas_call(functools.partial(kernel, n_slab, n_plane, rank), out_shap...  79.4 us
    broadcast_in_dim x1, other arithmetic, body(): return out.astype(F32)[None]  2.68 us

profile of v3, /device:TPU:25, one launch (start us, length us, event | category | flops | bytes accessed | tf_op | source)
XLA Modules:
  0.0 82.1 jit_solution(11553449513004974269)
XLA Ops:
  0.0 79.4 %sweep.1 = bf16[16,32768]{1,0:T(8,128)(2,1)} custom-call(f32[1,16,32768]{2,1,0:T(8,128)} %rs_ref.1, bf16[1,2,2048,2048]{3,2,1,0:T(8,128)(2,1)} %d_ref.1, bf16[1,2,96,2048]{3,2,1,0:T(8,128)(2,1)} %l_ref.1, bf16[1,2,96,2048]{3,2,1,0:T(8,128)(2,1)} %sf_ref.1, bf16[1,2,96,2048]{3,2,1,0:T(8,128)(2,1)} %t_ref.1), custom_call_target="tpu_custom_call" | custom-call | tf_op jit(solution)/shard_map/sweep/pallas_call | solution.py:395
  79.4 2.7 %bitcast_convert_fusion = f32[1,16,32768]{2,1,0:T(8,128)} fusion(bf16[16,32768]{1,0:T(8,128)(2,1)} %sweep.1), kind=kLoop, calls=%fused_computation | loop fusion | flops 524288 | bytes 3145728 | tf_op jit(solution)/shard_map/broadcast_in_dim | solution.py:426

commit v4 on v3

--- a/solution.py
+++ b/solution.py
@@ -14,6 +14,9 @@
 CHUNKS = 8
 X0, X1, T, RM, AM, B1, B2, C2, G2, G4, RS, V1, V2, V3, V4, VB, AV, E = range(18)
 N_GROUPS = 18
+FIRST, SECOND = 3, 5
+PLAN = (3, 2)
+EARLY_COMPOSITE = False
 
 
 def split(value):
@@ -111,28 +114,6 @@
         for k, q in targets:
             remote(src.at[k], dst, group, (slab, q)).start()
 
-    def rs_copy(k):
-        lanes = pl.ds(pl.multiple_of(device_at(k) * tile, tile), tile)
-        return pltpu.make_async_copy(rs_ref.at[0, :, lanes], rs_vm.at[k], rs_sem.at[k])
-
-    def start_rs(which):
-        def one(i, carry):
-            rs_copy(place(which, i)).start()
-            return carry
-        lax.fori_loop(0, side, one, 0)
-
-    start_rs(my_side)
-    s_copy = pltpu.make_async_copy(sf_ref.at[0], sw_vm.at[pl.ds(0, 2), pl.ds(0, rank), :], in_sem.at[1])
-    s_copy.start()
-
-    def d_copy(j):
-        rows = pl.ds(pl.multiple_of(j * step, step), step)
-        return pltpu.make_async_copy(d_ref.at[0, :, rows, :], d_vm.at[:, rows, :], d_sem.at[j])
-
-    def start_d(j, carry):
-        d_copy(j).start()
-        return carry
-
     u_recv[...] = jnp.zeros_like(u_recv)
     barrier = pltpu.get_barrier_semaphore()
 
@@ -146,6 +127,29 @@
     pl.when(s < n_slab - 1)(lambda: greet((s + 1, p)))
     for distance in (1, 2, 3, 4):
         pl.when(s >= distance)(functools.partial(lambda d: greet((s - d, p)), distance))
+
+
+    def rs_copy(k):
+        lanes = pl.ds(pl.multiple_of(device_at(k) * tile, tile), tile)
+        return pltpu.make_async_copy(rs_ref.at[0, :, lanes], rs_vm.at[k], rs_sem.at[k])
+
+    def start_rs(which):
+        def one(i, carry):
+            rs_copy(place(which, i)).start()
+            return carry
+        lax.fori_loop(0, side, one, 0)
+
+    start_rs(my_side)
+    s_copy = pltpu.make_async_copy(sf_ref.at[0], sw_vm.at[pl.ds(0, 2), pl.ds(0, rank), :], in_sem.at[1])
+    s_copy.start()
+
+    def d_copy(j):
+        rows = pl.ds(pl.multiple_of(j * step, step), step)
+        return pltpu.make_async_copy(d_ref.at[0, :, rows, :], d_vm.at[:, rows, :], d_sem.at[j])
+
+    def start_d(j, carry):
+        d_copy(j).start()
+        return carry
 
     start_rs(far_side)
     lax.fori_loop(0, CHUNKS, start_d, 0)
@@ -227,7 +231,9 @@
     s_copy.wait()
     l_copy.wait()
 
+    first, second = FIRST * side // 8, SECOND * side // 8
     pl.when(s >= 1)(t_copy.wait_send)
+    blocks_to(far[:first], x_send, x_recv.at[me], X1, s)
 
     @pl.when(s < n_slab - 1)
     def _():
@@ -237,8 +243,7 @@
 
         blocks_to(far + near + [(me, p)], m_part, m_recv.at[me], RM, s + 1)
 
-    first_batch = 5 * side // 8
-    blocks_to(far[:first_batch], x_send, x_recv.at[me], X1, s)
+    blocks_to(far[first:second], x_send, x_recv.at[me], X1, s)
     half_chunks = CHUNKS // 2
     pl.when(s < n_slab - 1)(lambda: trace_weights(0, half_chunks))
 
@@ -258,8 +263,12 @@
         pl.when(s + 1 < n_slab)(b1_copy.start)
         pl.when(s + 2 < n_slab)(b2_copy.start)
 
-    blocks_to(far[first_batch:], x_send, x_recv.at[me], X1, s)
+    blocks_to(far[second:], x_send, x_recv.at[me], X1, s)
     pl.when(s < n_slab - 1)(lambda: trace_weights(half_chunks, CHUNKS))
+
+    rank_part(my_side)
+    c_recv[me] = c_part[me]
+    blocks_to(near, c_part, c_recv.at[me], RS, s)
 
     @pl.when(s >= 1)
     def _():
@@ -273,32 +282,36 @@
         to_plane(a2.at[me], a2.at[me], G2)
         pl.when(s + 2 < n_slab)(c2_copy.start)
 
-    rank_part(my_side)
-    c_recv[me] = c_part[me]
-    blocks_to(near, c_part, c_recv.at[me], RS, s)
+    def longer_composites():
+        @pl.when(s >= 2)
+        def _():
+            await_recv(a2.at[others], G2)
+            keep(1, a2[...])
+
+        @pl.when(s >= 3)
+        def _():
+            await_recv(b2, B2)
+            a4[me, 0] = split_dot(b2[...], a_high[1], a_low[1])
+            a4[me, 1] = jnp.zeros(b2.shape, F32)
+
+            @pl.when(s >= 4)
+            def _():
+                await_recv(c2, C2)
+                a4[me, 1] = split_dot(c2[...], a_high[1], a_low[1])
+            to_plane(a4.at[me], a4.at[me], G4)
+
+    if EARLY_COMPOSITE:
+        longer_composites()
 
     await_recv(x_recv.at[all_far], X1)
     rank_part(far_side)
     blocks_to(far, c_part, c_recv.at[me], RS, s)
 
-    @pl.when(s >= 2)
-    def _():
-        await_recv(a2.at[others], G2)
-        keep(1, a2[...])
-
-    @pl.when(s >= 3)
-    def _():
-        await_recv(b2, B2)
-        a4[me, 0] = split_dot(b2[...], a_high[1], a_low[1])
-        a4[me, 1] = jnp.zeros(b2.shape, F32)
-
-        @pl.when(s >= 4)
-        def _():
-            await_recv(c2, C2)
-            a4[me, 1] = split_dot(c2[...], a_high[1], a_low[1])
-        to_plane(a4.at[me], a4.at[me], G4)
-
-    local_part(far_side, 0, half_chunks, False)
+    if not EARLY_COMPOSITE:
+        longer_composites()
+
+    before_sums, before_scan = PLAN[0], PLAN[0] + PLAN[1]
+    local_part(far_side, 0, before_sums, False)
     await_recv(c_recv.at[others], RS)
     u_send[...] = jnp.sum(c_recv[...], axis=0)
     u_copies = []
@@ -306,7 +319,7 @@
         copy = remote(u_send, u_recv.at[index], group, (s + index + 1, p))
         u_copies.append(copy)
         pl.when(s + index + 1 < n_slab)(copy.start)
-    local_part(far_side, half_chunks, CHUNKS, False)
+    local_part(far_side, before_sums, before_scan, False)
 
     @pl.when(s >= 3)
     def _():
@@ -330,6 +343,7 @@
         mix[me] = v_send[...] + split_dot(v_recv[...], a_high[3], a_low[3])
 
     to_plane(mix.at[me], mix.at[me], AV)
+    local_part(far_side, before_scan, CHUNKS, False)
     await_recv(mix.at[others], AV)
 
     mine = pl.ds(pl.multiple_of(p * tile, tile), tile)

time: 83.5 us -> 80.9 us (0.969); the launches traced: 82.1 us -> 80.4 us
  Pallas kernels: 79.4 us -> 77.7 us
    pallas_call x1, Pallas kernels: 79.4 us -> 77.7 us  [body(): pl.pallas_call(functools.partial(kernel, n_slab, n_plane, rank), out_shap...]
where the time goes in v4:
time: 80.9 us; the launch traced here: 80.4 us
  Pallas kernels  77.7 us (96%)
  other arithmetic  2.68 us (3%)
    pallas_call x1, Pallas kernels, body(): pl.pallas_call(functools.partial(kernel, n_slab, n_plane, rank), out_shap...  77.7 us
    broadcast_in_dim x1, other arithmetic, body(): return out.astype(F32)[None]  2.68 us

profile of v4, /device:TPU:25, one launch (start us, length us, event | category | flops | bytes accessed | tf_op | source)
XLA Modules:
  0.0 80.4 jit_solution(9145863960736159952)
XLA Ops:
  0.0 77.7 %sweep.1 = bf16[16,32768]{1,0:T(8,128)(2,1)} custom-call(f32[1,16,32768]{2,1,0:T(8,128)} %rs_ref.1, bf16[1,2,2048,2048]{3,2,1,0:T(8,128)(2,1)} %d_ref.1, bf16[1,2,96,2048]{3,2,1,0:T(8,128)(2,1)} %l_ref.1, bf16[1,2,96,2048]{3,2,1,0:T(8,128)(2,1)} %sf_ref.1, bf16[1,2,96,2048]{3,2,1,0:T(8,128)(2,1)} %t_ref.1), custom_call_target="tpu_custom_call" | custom-call | tf_op jit(solution)/shard_map/sweep/pallas_call | solution.py:409
  77.8 2.7 %bitcast_convert_fusion = f32[1,16,32768]{2,1,0:T(8,128)} fusion(bf16[16,32768]{1,0:T(8,128)(2,1)} %sweep.1), kind=kLoop, calls=%fused_computation | loop fusion | flops 524288 | bytes 3145728 | tf_op jit(solution)/shard_map/broadcast_in_dim | solution.py:440

commit v5 on v4

--- a/solution.py
+++ b/solution.py
@@ -12,11 +12,10 @@
 BF16 = jnp.bfloat16
 PAD = 128
 CHUNKS = 8
-X0, X1, T, RM, AM, B1, B2, C2, G2, G4, RS, V1, V2, V3, V4, VB, AV, E = range(18)
-N_GROUPS = 18
-FIRST, SECOND = 3, 5
-PLAN = (3, 2)
-EARLY_COMPOSITE = False
+X0, X1, T, RM, AM, RS, AV, E, U, MH, MS = 0, 1, 2, 3, 4, 5, 6, 7, 8, 15, 22
+N_GROUPS = 29
+FIRST = 5
+PLAN = (2, 3)
 
 
 def split(value):
@@ -40,29 +39,26 @@
     return jnp.concatenate([real, imag], axis=1)
 
 
-def expanded(top):
-    real, imag = top[:, :PAD], top[:, PAD:]
-    return jnp.concatenate([top, jnp.concatenate([-imag, real], axis=1)], axis=0)
+def moved(rows, *parts):
+    count = rows.shape[0]
+    upright = jnp.concatenate([rows[:, :PAD], rows[:, PAD:]], axis=0)
+    stacked = stacked_halves(upright)
+    both = sum(nn_dot(stacked, part) for part in parts)
+    both = both[:2 * count] + both[2 * count:]
+    return from_products(both)
 
 
 def stacked_halves(rows):
     rows_high = rows.astype(BF16).astype(F32)
     return jnp.concatenate([rows_high, rows - rows_high], axis=0).astype(BF16)
-
-
-def split_dot(rows, high, low):
-    count = rows.shape[0]
-    stacked = stacked_halves(rows)
-    total = nn_dot(stacked, high) + nn_dot(stacked, low)
-    return total[:count] + total[count:]
 
 
 def kernel(
     n_slab, n_plane, rank,
     rs_ref, d_ref, l_ref, sf_ref, t_ref, o_ref,
     d_vm, rs_vm, x_send, x_recv, t_vm, l_vm, sw_vm, local, e_send,
-    m_part, m_recv, a1, a2, a4, b1, b2, c2, a_high, a_low,
-    c_part, c_recv, u_send, u_recv, v_send, v_recv, mix,
+    m_part, m_recv, a1, earlier,
+    c_part, c_recv, u_send, u_recv, mix,
     d_sem, rs_sem, in_sem, own_sem, send_sem, recv_sem,
 ):
     s = lax.axis_index("slab")
@@ -103,6 +99,16 @@
         remote(ref, ref, group, peer).wait_send()
 
     others = pl.ds(0, n_plane - 1)
+    held = m_part.shape[1]
+    n_owners = rank // held
+    spread = [2 * i for i in range(3)] + [side + 2 * i for i in range(1, 4)]
+    owner_places = spread if n_plane == 16 else list(range(n_owners))
+    owner_devices = [(k % side) // run * 2 * run + k // side * run + k % side % run for k in owner_places]
+    owner, my_rows = me < 0, jnp.int32(0)
+    for j, k in enumerate(owner_places):
+        owner = owner | (me == k)
+        my_rows = my_rows + j * (me == k).astype(jnp.int32)
+    all_rows = pl.ds(0, n_owners)
     near_others = pl.ds(0, side - 1)
     all_far = pl.ds(0, side)
 
@@ -114,7 +120,11 @@
         for k, q in targets:
             remote(src.at[k], dst, group, (slab, q)).start()
 
-    u_recv[...] = jnp.zeros_like(u_recv)
+    for slot in range(2):
+        a1[slot, n_owners:] = jnp.zeros(a1.shape[1:], BF16)[n_owners:]
+    for slot in range(n_slab - 1):
+        for part in range(2):
+            earlier[slot, part, n_owners:] = jnp.zeros(a1.shape[1:], BF16)[n_owners:]
     barrier = pltpu.get_barrier_semaphore()
 
     def greet(device):
@@ -125,7 +135,7 @@
         return carry
     lax.fori_loop(1, n_plane, greet_plane, 0)
     pl.when(s < n_slab - 1)(lambda: greet((s + 1, p)))
-    for distance in (1, 2, 3, 4):
+    for distance in range(1, n_slab):
         pl.when(s >= distance)(functools.partial(lambda d: greet((s - d, p)), distance))
 
 
@@ -158,15 +168,13 @@
     for padded in (t_vm, l_vm, sw_vm):
         padded[pl.ds(0, 2), rank:, :] = jnp.zeros((2, PAD - rank, tile), BF16)
 
-    a_high[...] = jnp.zeros_like(a_high)
-    a_low[...] = jnp.zeros_like(a_low)
 
     @pl.when(s == n_slab - 1)
     def _():
         sw_vm[pl.ds(2, 4)] = jnp.zeros((4, PAD, tile), BF16)
 
     expected = n_plane - 1 + (s >= 1).astype(jnp.int32)
-    for distance in (1, 2, 3, 4):
+    for distance in range(1, n_slab):
         expected = expected + (s + distance < n_slab).astype(jnp.int32)
     pl.semaphore_wait(barrier, expected)
 
@@ -196,8 +204,8 @@
                 d_copy(j).wait()
             rows = pl.ds(pl.multiple_of(j * step, step), step)
             x = x_recv[side_rows(which)].reshape(side * 16, tile)
-            real = nt_dot(x, d_vm[0, rows, :])
-            imag = nt_dot(x, d_vm[1, rows, :])
+            real = nt_dot(d_vm[0, rows, :], x).T
+            imag = nt_dot(d_vm[1, rows, :], x).T
             local[which, :side * 8, rows] = real[:side * 8] - imag[side * 8:]
             local[which, side * 8:, rows] = real[side * 8:] + imag[:side * 8]
             return carry
@@ -231,7 +239,7 @@
     s_copy.wait()
     l_copy.wait()
 
-    first, second = FIRST * side // 8, SECOND * side // 8
+    first = FIRST * side // 8
     pl.when(s >= 1)(t_copy.wait_send)
     blocks_to(far[:first], x_send, x_recv.at[me], X1, s)
 
@@ -241,106 +249,86 @@
         products = nt_dot(l_vm[...].reshape(2 * PAD, tile), t_vm[...].reshape(2 * PAD, tile))
         m_part[...] = from_products(products).reshape(m_part.shape)
 
-        blocks_to(far + near + [(me, p)], m_part, m_recv.at[me], RM, s + 1)
-
-    blocks_to(far[first:second], x_send, x_recv.at[me], X1, s)
-    half_chunks = CHUNKS // 2
-    pl.when(s < n_slab - 1)(lambda: trace_weights(0, half_chunks))
-
-    def keep(index, top):
-        high, low = split(expanded(top.reshape(PAD, 2 * PAD)))
-        a_high[index] = high
-        a_low[index] = low
-
-    b1_copy = remote(a1.at[me], b1, B1, (s + 1, p))
-    b2_copy = remote(a1.at[me], b2, B2, (s + 2, p))
-    c2_copy = remote(a2.at[me], c2, C2, (s + 2, p))
-    @pl.when(s >= 1)
+        for j, q in enumerate(owner_devices):
+            remote(m_part.at[j], m_recv.at[me], RM, (s + 1, q)).start()
+
+    blocks_to(far[first:], x_send, x_recv.at[me], X1, s)
+    pl.when(s < n_slab - 1)(lambda: trace_weights(0, CHUNKS))
+
+    @pl.when((s >= 1) & owner)
     def _():
         await_recv(m_recv, RM)
-        a1[me] = jnp.sum(m_recv[...], axis=0)
-        to_plane(a1.at[me], a1.at[me], AM)
-        pl.when(s + 1 < n_slab)(b1_copy.start)
-        pl.when(s + 2 < n_slab)(b2_copy.start)
-
-    blocks_to(far[second:], x_send, x_recv.at[me], X1, s)
-    pl.when(s < n_slab - 1)(lambda: trace_weights(half_chunks, CHUNKS))
+        high, low = split(jnp.sum(m_recv[...], axis=0))
+        a1[0, my_rows] = high
+        a1[1, my_rows] = low
+        to_plane(a1.at[:, my_rows], a1.at[:, my_rows], AM)
 
     rank_part(my_side)
     c_recv[me] = c_part[me]
     blocks_to(near, c_part, c_recv.at[me], RS, s)
 
-    @pl.when(s >= 1)
-    def _():
-        await_recv(a1.at[others], AM)
-        keep(0, a1[...])
-
-    @pl.when(s >= 2)
-    def _():
-        await_recv(b1, B1)
-        a2[me] = split_dot(b1[...], a_high[0], a_low[0])
-        to_plane(a2.at[me], a2.at[me], G2)
-        pl.when(s + 2 < n_slab)(c2_copy.start)
-
-    def longer_composites():
-        @pl.when(s >= 2)
+    part = lax.rem(p, 2)
+    partner = (s, p + 1 - 2 * part)
+    later_copies = [
+        (
+            remote(a1.at[part, all_rows], earlier.at[d - 1, part, all_rows], MH + d - 1, (s + d, p)),
+            (s >= 1) & (s + d < n_slab),
+        )
+        for d in range(1, n_slab)
+    ]
+    shared_copies = [
+        remote(earlier.at[d - 1, part, all_rows], earlier.at[d - 1, part, all_rows], MS + d - 1, partner)
+        for d in range(1, n_slab)
+    ]
+
+    def send_later():
+        @pl.when(s >= 1)
         def _():
-            await_recv(a2.at[others], G2)
-            keep(1, a2[...])
-
-        @pl.when(s >= 3)
-        def _():
-            await_recv(b2, B2)
-            a4[me, 0] = split_dot(b2[...], a_high[1], a_low[1])
-            a4[me, 1] = jnp.zeros(b2.shape, F32)
-
-            @pl.when(s >= 4)
-            def _():
-                await_recv(c2, C2)
-                a4[me, 1] = split_dot(c2[...], a_high[1], a_low[1])
-            to_plane(a4.at[me], a4.at[me], G4)
-
-    if EARLY_COMPOSITE:
-        longer_composites()
+            pl.when(owner)(lambda: await_recv(a1.at[:, pl.ds(0, n_owners - 1)], AM))
+            pl.when(jnp.logical_not(owner))(lambda: await_recv(a1.at[:, all_rows], AM))
+            for copy, needed in later_copies:
+                pl.when(needed)(copy.start)
 
     await_recv(x_recv.at[all_far], X1)
     rank_part(far_side)
     blocks_to(far, c_part, c_recv.at[me], RS, s)
 
-    if not EARLY_COMPOSITE:
-        longer_composites()
+    send_later()
 
     before_sums, before_scan = PLAN[0], PLAN[0] + PLAN[1]
     local_part(far_side, 0, before_sums, False)
     await_recv(c_recv.at[others], RS)
     u_send[...] = jnp.sum(c_recv[...], axis=0)
     u_copies = []
-    for index, group in enumerate((V1, V2, V3, V4)):
-        copy = remote(u_send, u_recv.at[index], group, (s + index + 1, p))
+    for distance in range(1, n_slab):
+        copy = remote(u_send, u_recv.at[distance - 1], U + distance - 1, (s + distance, p))
         u_copies.append(copy)
-        pl.when(s + index + 1 < n_slab)(copy.start)
+        pl.when(s + distance < n_slab)(copy.start)
     local_part(far_side, before_sums, before_scan, False)
-
-    @pl.when(s >= 3)
+    for d in range(1, n_slab - 1):
+        @pl.when(s > d)
+        def _():
+            later_copies[d - 1][0].wait_recv()
+            shared_copies[d - 1].start()
+
+    def await_u(distance):
+        remote(u_send, u_recv.at[0], U + distance - 1, peer).wait_recv()
+
+    mix[me] = u_send[0]
+
+    @pl.when(s >= 1)
     def _():
-        await_recv(a4.at[others], G4)
-        keep(2, a4[:, 0])
-        keep(3, a4[:, 1])
-
-    for index in range(4):
-        pl.when(s > index)(u_copies[index].wait_recv)
-    total = u_send[0] + u_recv[0, 1]
-    for index in range(3):
-        total = total + split_dot(u_recv[index, 0] + u_recv[index + 1, 1], a_high[index], a_low[index])
-    v_send[...] = total
-    mix[me] = total
-    v_copy = remote(v_send, v_recv, VB, (s + 4, p))
-    pl.when(s + 4 < n_slab)(v_copy.start)
-
-    @pl.when(s >= 4)
-    def _():
-        v_copy.wait_recv()
-        mix[me] = v_send[...] + split_dot(v_recv[...], a_high[3], a_low[3])
+        await_u(s)
+
+        def advance(step_back, value):
+            d = s - step_back
+            await_u(d)
+            remote(a1.at[0, all_rows], earlier.at[0, 0, all_rows], MS + d - 1, peer).wait_recv()
+            high, low = earlier[d - 1, 0].reshape(PAD, 2 * PAD), earlier[d - 1, 1].reshape(PAD, 2 * PAD)
+            return u_recv[d - 1, 0] + u_recv[d, 1] + moved(value, high, low)
+        value = lax.fori_loop(1, s, advance, u_recv[s - 1, 0])
+        high, low = a1[0].reshape(PAD, 2 * PAD), a1[1].reshape(PAD, 2 * PAD)
+        mix[me] = u_send[0] + u_recv[0, 1] + moved(value, high, low)
 
     to_plane(mix.at[me], mix.at[me], AV)
     local_part(far_side, before_scan, CHUNKS, False)
@@ -372,22 +360,15 @@
 
     @pl.when(s < n_slab - 1)
     def _():
-        await_send(m_part, RM)
-
-    @pl.when(s >= 1)
-    def _():
-        await_send(a1.at[others], AM)
-        pl.when(s + 1 < n_slab)(b1_copy.wait_send)
-        pl.when(s + 2 < n_slab)(b2_copy.wait_send)
-
-    @pl.when(s >= 2)
-    def _():
-        await_send(a2.at[others], G2)
-        pl.when(s + 2 < n_slab)(c2_copy.wait_send)
-    pl.when(s >= 3)(lambda: await_send(a4.at[others], G4))
-    for index in range(4):
-        pl.when(s + index + 1 < n_slab)(u_copies[index].wait_send)
-    pl.when(s + 4 < n_slab)(v_copy.wait_send)
+        await_send(m_part.at[all_rows], RM)
+
+    pl.when((s >= 1) & owner)(lambda: await_send(m_recv.at[others], AM))
+    for copy, needed in later_copies:
+        pl.when(needed)(copy.wait_send)
+    for d in range(1, n_slab - 1):
+        pl.when(s > d)(shared_copies[d - 1].wait_send)
+    for distance in range(1, n_slab):
+        pl.when(s + distance < n_slab)(u_copies[distance - 1].wait_send)
     own.wait()
     await_send(e_send.at[others], E)
     await_recv(o_ref.at[:, pl.ds(0, (n_plane - 1) * tile)], E)
@@ -399,13 +380,10 @@
     def body(right_sides, diag_tiles, left_factors, source_factors, trace_factors):
         tile, rank = diag_tiles.shape[2], left_factors.shape[2]
         columns = right_sides.shape[1]
-        part = PAD // n_plane
+        held = 16 if n_plane == 16 else 32
         pairs = pltpu.VMEM((n_plane, 2, 8, 2 * PAD), F32)
-        ranks = pltpu.VMEM((n_plane, part, 2 * PAD), F32)
-        one = pltpu.VMEM((part, 2 * PAD), F32)
         padded = pltpu.VMEM((2, PAD, tile), BF16)
         blocks = pltpu.VMEM((n_plane, columns, tile), BF16)
-        squares = pltpu.VMEM((4, 2 * PAD, 2 * PAD), BF16)
         out = pl.pallas_call(
             functools.partial(kernel, n_slab, n_plane, rank),
             out_shape=jax.ShapeDtypeStruct((columns, n_plane * tile), BF16),
@@ -417,13 +395,13 @@
                 blocks, blocks, padded, padded, pltpu.VMEM((6, PAD, tile), BF16),
                 pltpu.VMEM((2, columns * n_plane // 2, tile), F32),
                 blocks,
-                ranks, ranks, ranks, ranks, pltpu.VMEM((n_plane, 2, part, 2 * PAD), F32),
-                one, one, one, squares, squares,
+                pltpu.VMEM((PAD // held, held, 2 * PAD), F32),
+                pltpu.VMEM((n_plane, held, 2 * PAD), F32),
+                pltpu.VMEM((2, PAD // held, held, 2 * PAD), BF16),
+                pltpu.VMEM((n_slab - 1, 2, PAD // held, held, 2 * PAD), BF16),
                 pairs, pairs,
                 pltpu.VMEM((2, 8, 2 * PAD), F32),
-                pltpu.VMEM((4, 2, 8, 2 * PAD), F32),
-                pltpu.VMEM((8, 2 * PAD), F32),
-                pltpu.VMEM((8, 2 * PAD), F32),
+                pltpu.VMEM((n_slab - 1, 2, 8, 2 * PAD), F32),
                 pltpu.VMEM((n_plane, 8, 2 * PAD), F32),
                 pltpu.SemaphoreType.DMA((CHUNKS,)),
                 pltpu.SemaphoreType.DMA((n_plane,)),

time: 80.9 us -> 78.3 us (0.968)
  Pallas kernels: 77.7 us -> 74.9 us
    pallas_call x1, Pallas kernels: 77.7 us -> 74.9 us  [body(): pl.pallas_call(functools.partial(kernel, n_slab, n_plane, rank), out_shap...]
where the time goes in v5:
time: 78.3 us; the launch traced here: 77.6 us
  Pallas kernels  74.9 us (96%)
  other arithmetic  2.68 us (3%)
    pallas_call x1, Pallas kernels, body(): pl.pallas_call(functools.partial(kernel, n_slab, n_plane, rank), out_shap...  74.9 us
    broadcast_in_dim x1, other arithmetic, body(): return out.astype(F32)[None]  2.68 us

profile of v5, /device:TPU:25, one launch (start us, length us, event | category | flops | bytes accessed | tf_op | source)
XLA Modules:
  0.0 77.6 jit_solution(3315157316115531470)
XLA Ops:
  0.0 74.9 %sweep.1 = bf16[16,32768]{1,0:T(8,128)(2,1)} custom-call(f32[1,16,32768]{2,1,0:T(8,128)} %rs_ref.1, bf16[1,2,2048,2048]{3,2,1,0:T(8,128)(2,1)} %d_ref.1, bf16[1,2,96,2048]{3,2,1,0:T(8,128)(2,1)} %l_ref.1, bf16[1,2,96,2048]{3,2,1,0:T(8,128)(2,1)} %sf_ref.1, bf16[1,2,96,2048]{3,2,1,0:T(8,128)(2,1)} %t_ref.1), custom_call_target="tpu_custom_call" | custom-call | tf_op jit(solution)/shard_map/sweep/pallas_call | solution.py:387
  74.9 2.7 %bitcast_convert_fusion = f32[1,16,32768]{2,1,0:T(8,128)} fusion(bf16[16,32768]{1,0:T(8,128)(2,1)} %sweep.1), kind=kLoop, calls=%fused_computation | loop fusion | flops 524288 | bytes 3145728 | tf_op jit(solution)/shard_map/broadcast_in_dim | solution.py:418

commit v6 on v5

--- a/solution.py
+++ b/solution.py
@@ -14,8 +14,7 @@
 CHUNKS = 8
 X0, X1, T, RM, AM, RS, AV, E, U, MH, MS = 0, 1, 2, 3, 4, 5, 6, 7, 8, 15, 22
 N_GROUPS = 29
-FIRST = 5
-PLAN = (2, 3)
+PLAN = (1, 3)
 
 
 def split(value):
@@ -56,7 +55,7 @@
 def kernel(
     n_slab, n_plane, rank,
     rs_ref, d_ref, l_ref, sf_ref, t_ref, o_ref,
-    d_vm, rs_vm, x_send, x_recv, t_vm, l_vm, sw_vm, local, e_send,
+    d_vm, rs_vm, x_send, x_recv, t_own, t_vm, l_vm, sw_vm, local, e_send,
     m_part, m_recv, a1, earlier,
     c_part, c_recv, u_send, u_recv, mix,
     d_sem, rs_sem, in_sem, own_sem, send_sem, recv_sem,
@@ -120,11 +119,9 @@
         for k, q in targets:
             remote(src.at[k], dst, group, (slab, q)).start()
 
-    for slot in range(2):
-        a1[slot, n_owners:] = jnp.zeros(a1.shape[1:], BF16)[n_owners:]
-    for slot in range(n_slab - 1):
-        for part in range(2):
-            earlier[slot, part, n_owners:] = jnp.zeros(a1.shape[1:], BF16)[n_owners:]
+    own_t = pltpu.make_async_copy(t_ref.at[0], t_own, in_sem.at[2])
+    own_t.start()
+
     barrier = pltpu.get_barrier_semaphore()
 
     def greet(device):
@@ -173,12 +170,19 @@
     def _():
         sw_vm[pl.ds(2, 4)] = jnp.zeros((4, PAD, tile), BF16)
 
+    for slot in range(2):
+        a1[slot, n_owners:] = jnp.zeros(a1.shape[1:], BF16)[n_owners:]
+    for slot in range(n_slab - 1):
+        for part in range(2):
+            earlier[slot, part, n_owners:] = jnp.zeros(a1.shape[1:], BF16)[n_owners:]
+
     expected = n_plane - 1 + (s >= 1).astype(jnp.int32)
     for distance in range(1, n_slab):
         expected = expected + (s + distance < n_slab).astype(jnp.int32)
     pl.semaphore_wait(barrier, expected)
 
-    t_copy = remote(t_ref.at[0], t_vm.at[:, pl.ds(0, rank), :], T, (s - 1, p))
+    own_t.wait()
+    t_copy = remote(t_own, t_vm.at[:, pl.ds(0, rank), :], T, (s - 1, p))
     pl.when(s >= 1)(t_copy.start)
 
     for k, q in near:
@@ -239,9 +243,8 @@
     s_copy.wait()
     l_copy.wait()
 
-    first = FIRST * side // 8
     pl.when(s >= 1)(t_copy.wait_send)
-    blocks_to(far[:first], x_send, x_recv.at[me], X1, s)
+    blocks_to(far, x_send, x_recv.at[me], X1, s)
 
     @pl.when(s < n_slab - 1)
     def _():
@@ -252,20 +255,21 @@
         for j, q in enumerate(owner_devices):
             remote(m_part.at[j], m_recv.at[me], RM, (s + 1, q)).start()
 
-    blocks_to(far[first:], x_send, x_recv.at[me], X1, s)
     pl.when(s < n_slab - 1)(lambda: trace_weights(0, CHUNKS))
 
-    @pl.when((s >= 1) & owner)
-    def _():
-        await_recv(m_recv, RM)
-        high, low = split(jnp.sum(m_recv[...], axis=0))
-        a1[0, my_rows] = high
-        a1[1, my_rows] = low
-        to_plane(a1.at[:, my_rows], a1.at[:, my_rows], AM)
+    def sum_m():
+        @pl.when((s >= 1) & owner)
+        def _():
+            await_recv(m_recv, RM)
+            high, low = split(jnp.sum(m_recv[...], axis=0))
+            a1[0, my_rows] = high
+            a1[1, my_rows] = low
+            to_plane(a1.at[:, my_rows], a1.at[:, my_rows], AM)
 
     rank_part(my_side)
     c_recv[me] = c_part[me]
     blocks_to(near, c_part, c_recv.at[me], RS, s)
+    sum_m()
 
     part = lax.rem(p, 2)
     partner = (s, p + 1 - 2 * part)
@@ -392,7 +396,7 @@
             scratch_shapes=[
                 pltpu.VMEM((2, tile, tile), BF16),
                 pltpu.VMEM((n_plane, columns, tile), F32),
-                blocks, blocks, padded, padded, pltpu.VMEM((6, PAD, tile), BF16),
+                blocks, blocks, pltpu.VMEM((2, rank, tile), BF16), padded, padded, pltpu.VMEM((6, PAD, tile), BF16),
                 pltpu.VMEM((2, columns * n_plane // 2, tile), F32),
                 blocks,
                 pltpu.VMEM((PAD // held, held, 2 * PAD), F32),
@@ -405,7 +409,7 @@
                 pltpu.VMEM((n_plane, 8, 2 * PAD), F32),
                 pltpu.SemaphoreType.DMA((CHUNKS,)),
                 pltpu.SemaphoreType.DMA((n_plane,)),
-                pltpu.SemaphoreType.DMA((2,)),
+                pltpu.SemaphoreType.DMA((3,)),
                 pltpu.SemaphoreType.DMA,
                 pltpu.SemaphoreType.DMA((N_GROUPS,)),
                 pltpu.SemaphoreType.DMA((N_GROUPS,)),

time: 78.3 us -> 79.5 us (1.015)
  Pallas kernels: 74.9 us -> 76 us
    pallas_call x1, Pallas kernels: 74.9 us -> 76 us  [body(): pl.pallas_call(functools.partial(kernel, n_slab, n_plane, rank), out_shap...]
where the time goes in v6:
time: 79.5 us; the launch traced here: 78.7 us
  Pallas kernels  76 us (96%)
  other arithmetic  2.68 us (3%)
    pallas_call x1, Pallas kernels, body(): pl.pallas_call(functools.partial(kernel, n_slab, n_plane, rank), out_shap...  76 us
    broadcast_in_dim x1, other arithmetic, body(): return out.astype(F32)[None]  2.68 us

profile of v6, /device:TPU:25, one launch (start us, length us, event | category | flops | bytes accessed | tf_op | source)
XLA Modules:
  0.0 78.7 jit_solution(14213084126837108394)
XLA Ops:
  0.0 76.0 %sweep.1 = bf16[16,32768]{1,0:T(8,128)(2,1)} custom-call(f32[1,16,32768]{2,1,0:T(8,128)} %rs_ref.1, bf16[1,2,2048,2048]{3,2,1,0:T(8,128)(2,1)} %d_ref.1, bf16[1,2,96,2048]{3,2,1,0:T(8,128)(2,1)} %l_ref.1, bf16[1,2,96,2048]{3,2,1,0:T(8,128)(2,1)} %sf_ref.1, bf16[1,2,96,2048]{3,2,1,0:T(8,128)(2,1)} %t_ref.1), custom_call_target="tpu_custom_call" | custom-call | tf_op jit(solution)/shard_map/sweep/pallas_call | solution.py:391
  76.1 2.7 %bitcast_convert_fusion = f32[1,16,32768]{2,1,0:T(8,128)} fusion(bf16[16,32768]{1,0:T(8,128)(2,1)} %sweep.1), kind=kLoop, calls=%fused_computation | loop fusion | flops 524288 | bytes 3145728 | tf_op jit(solution)/shard_map/broadcast_in_dim | solution.py:422
